TPU v7x, 32 devices: a whole 2x2x4 slice. The times are simulated.
32 devices in a mesh: gx: 4 (over y, x), gy: 8 (over z, core).
Axes of the slice: x: 2, y: 2, z: 4, core: 2. Of those that a mesh axis runs over, the one named last changes fastest.
Arguments:
- velocity: float32 [3, 2, 512, 1024], P(None, None, 'gx', 'gy'), may hold values from -8 to 8
- diffusion: float32 [2, 512, 1024], P(None, 'gx', 'gy'), may hold values from 16384 to 262144
Outputs:
- new_velocity: float32 [3, 2, 512, 1024], P(None, None, 'gx', 'gy')
All inputs are finite; a program needn't handle non-finite values.
Results may differ from a plain program's by a relative error of at most 0.000024.
Values sent between devices are 32-bit elements; how exact they have to be, the bound alone decides.
A program may use at most 64 MiB of HBM per device.

v0:
```python
import jax
import jax.numpy as jnp
from jax import lax
from jax.sharding import PartitionSpec as P

courant = 0.25


def prefix_2(part, axis, combine, identity, reverse):
    count = lax.axis_size(axis)
    place = lax.axis_index(axis)
    ahead = count - 1 - place if reverse else place
    gathered = jax.tree.map(lambda a: lax.all_gather(a, axis), part)
    state = jax.tree.map(lambda a, e: jnp.zeros_like(a) + jnp.asarray(e, a.dtype), part, identity)

    def one(hop, state):
        source = count - 1 - hop if reverse else hop
        return combine(
            state, jax.tree.map(lambda a: lax.dynamic_index_in_dim(a, source, 0, False), gathered)
        )

    return lax.fori_loop(0, ahead, one, state)


def padded_2(block, sides, width):
    for axis, dim in sides:
        count = lax.axis_size(axis)
        forward = [(i, i + 1) for i in range(count - 1)]
        backward = [(target, source) for source, target in forward]
        low = lax.ppermute(
            lax.slice_in_dim(block, block.shape[dim] - width, None, axis=dim), axis, forward
        )
        high = lax.ppermute(lax.slice_in_dim(block, 0, width, axis=dim), axis, backward)
        block = jnp.concatenate([low, block, high], axis=dim)
    return block


def compose(former, latter):
    top_left = latter[0] * former[0] + latter[1] * former[2]
    top_right = latter[0] * former[1] + latter[1] * former[3]
    low_left = latter[2] * former[0] + latter[3] * former[2]
    low_right = latter[2] * former[1] + latter[3] * former[3]
    carried = latter[4] * former[4]
    row_first = latter[5] * former[0] + latter[6] * former[2] + latter[4] * former[5]
    row_second = latter[5] * former[1] + latter[6] * former[3] + latter[4] * former[6]
    factor = 1.0 / (jnp.abs(top_left) + jnp.abs(top_right) + jnp.abs(low_left) + jnp.abs(low_right))
    return (
        top_left * factor,
        top_right * factor,
        low_left * factor,
        low_right * factor,
        carried * factor,
        row_first * factor,
        row_second * factor,
    )


def combine_affine(former, latter):
    return (latter[0] * former[0], latter[0] * former[1] + latter[1])


def neutral_of(shape):
    ones = jnp.ones(shape, jnp.float32)
    zeros = jnp.zeros(shape, jnp.float32)
    return (ones, zeros, zeros, ones, ones, zeros, zeros)


def forward(source, lower_face, upper_face):

    def advance(carry, entries):
        low_now, high_now, src_now = entries
        below = jnp.broadcast_to(low_now[None], src_now.shape)
        above = jnp.broadcast_to(high_now[None], src_now.shape)
        element = (
            below,
            jnp.ones_like(src_now),
            below,
            1.0 + above,
            below,
            jnp.zeros_like(src_now),
            src_now,
        )
        joined = compose(carry, element)
        return (joined, joined)

    unused, prefix = lax.scan(
        advance, neutral_of(source.shape[1:]), (lower_face, upper_face, source), unroll=8
    )
    return prefix


def eliminate(prefix, share_in, value_in):
    numer = prefix[0] * share_in + prefix[1]
    denom = prefix[2] * share_in + prefix[3]
    upper_q = prefix[5] * share_in + prefix[6] + prefix[4] * value_in
    return (numer / denom, upper_q / denom)


def backward(keep_part, value_part):

    def retreat(carry, entries):
        keep_now, value_now = entries
        slope = keep_now * carry[0]
        offset = value_now + keep_now * carry[1]
        return ((slope, offset), (slope, offset))

    start = (
        jnp.ones(keep_part.shape[1:], jnp.float32),
        jnp.zeros(keep_part.shape[1:], jnp.float32),
    )
    unused, suffix = lax.scan(retreat, start, (keep_part, value_part), reverse=True, unroll=8)
    return suffix


def entering(before):
    scale_in = before[2] + before[3]
    return ((before[0] + before[1]) / scale_in, (before[5] + before[6]) / scale_in)


def chain_x(source, lower_face, upper_face):
    prefix = forward(source, lower_face, upper_face)
    ends = tuple((leaf[-1] for leaf in prefix))
    before = prefix_2(
        (ends[0], ends[1], ends[2], ends[3], ends[4], ends[5], ends[6]),
        "gx",
        compose,
        neutral_of(ends[0].shape),
        False,
    )
    share_in, value_in = entering(before)
    share, value = eliminate(prefix, share_in, value_in)
    suffix = backward(1.0 - share, value)
    starts = (suffix[0][0], suffix[1][0])
    behind = prefix_2(
        (starts[0], starts[1]),
        "gx",
        combine_affine,
        (jnp.ones_like(starts[0]), jnp.zeros_like(starts[1])),
        True,
    )
    return suffix[0] * behind[1][None] + suffix[1]


def chain_y(source, lower_face, upper_face):
    prefix = forward(source, lower_face, upper_face)
    ends = tuple((leaf[-1] for leaf in prefix))
    before = prefix_2(
        (ends[0], ends[1], ends[2], ends[3], ends[4], ends[5], ends[6]),
        "gy",
        compose,
        neutral_of(ends[0].shape),
        False,
    )
    share_in, value_in = entering(before)
    share, value = eliminate(prefix, share_in, value_in)
    suffix = backward(1.0 - share, value)
    starts = (suffix[0][0], suffix[1][0])
    behind = prefix_2(
        (starts[0], starts[1]),
        "gy",
        combine_affine,
        (jnp.ones_like(starts[0]), jnp.zeros_like(starts[1])),
        True,
    )
    return suffix[0] * behind[1][None] + suffix[1]


def local(velocity, diffusion):
    stacked = jnp.concatenate([velocity, diffusion[None]], 0)
    padded = padded_2(stacked, (("gx", 2), ("gy", 3)), 1)
    grad_x = padded[:3, :, 2:, 1:-1] - padded[:3, :, :-2, 1:-1]
    grad_y = padded[:3, :, 1:-1, 2:] - padded[:3, :, 1:-1, :-2]
    source = velocity - 0.5 * courant * (velocity[0] * grad_x + velocity[1] * grad_y)
    viscous = padded[3]
    lower_x = 0.5 * (viscous[:, :-2, 1:-1] + diffusion)
    upper_x = 0.5 * (viscous[:, 2:, 1:-1] + diffusion)
    lower_y = 0.5 * (viscous[:, 1:-1, :-2] + diffusion)
    upper_y = 0.5 * (viscous[:, 1:-1, 2:] + diffusion)
    source_lead = jnp.transpose(source, (2, 0, 1, 3))
    lower_xl = jnp.transpose(lower_x, (1, 0, 2))
    upper_xl = jnp.transpose(upper_x, (1, 0, 2))
    lower_yl = jnp.transpose(lower_y, (2, 0, 1))
    upper_yl = jnp.transpose(upper_y, (2, 0, 1))
    middle = chain_x(source_lead, lower_xl, upper_xl)
    middle_lead = jnp.transpose(middle, (3, 1, 2, 0))
    result = chain_y(middle_lead, lower_yl, upper_yl)
    return jnp.transpose(result, (1, 2, 3, 0))


def solution(mesh):
    in_specs = (P(None, None, "gx", "gy"), P(None, "gx", "gy"))
    out_specs = P(None, None, "gx", "gy")
    return jax.shard_map(local, mesh=mesh, in_specs=in_specs, out_specs=out_specs, check_vma=False)
```

profile of v0, /device:TPU:0, one launch (start us, length us, event | category | flops | bytes accessed | tf_op | source)
XLA Modules:
  0.0 389.9 jit_solution(11397489688633304800)
XLA Ops:
  0.9 4.8 %collective-permute-start = (f32[4,2,1,128]{3,2,1,0:T(1,128)S(1)}, f32[4,2,1,128]{3,2,1,0:T(1,128)S(1)}, u32[]{:S(2)}, u32[]{:S(2)}) collective-permute-start(f32[4,2,1,128]{3,2,1,0:T(1,128)S(1)} %get-tuple-element.1857), channel_id=1, source_target_pairs={{0,8},{8,16},{16,24},{1,9},{9,17},{17,25},{2,10},{10,18},{18,26},{... | collective-permute-start | bytes 12296 | tf_op jit(solution)/shard_map/ppermute | solution.py:30
  5.7 1.3 collective-permute-start.1
  7.0 4.2 %collective-permute-done.1 = f32[4,2,1,128]{3,2,1,0:T(1,128)S(1)} collective-permute-done((f32[4,2,1,128]{3,2,1,0:T(1,128)S(1)}, f32[4,2,1,128]{3,2,1,0:T(1,128)S(1)}, u32[]{:S(2)}, u32[]{:S(2)}) %collective-permute-start.1) | collective-permute-done | bytes 4128 | tf_op jit(solution)/shard_map/ppermute | solution.py:33
  11.8 1.3 collective-permute-start.2
  13.4 1.3 collective-permute-start.3
  15.2 3.1 collective-permute-done.3
  20.8 89.3 %while.192 = (s32[]{:T(128)}, f32[3,2,128]{2,1,0:T(2,128)S(1)}, f32[3,2,128]{2,1,0:T(2,128)S(1)}, f32[3,2,128]{2,1,0:T(2,128)S(1)}, f32[3,2,128]{2,1,0:T(2,128)S...) while((s32[]{:T(128)}, f32[3,2,128]{2,1,0:T(2,128)S(1)}, ...), condition=%wide.region_1.2_spmd.clone, body=%wide.region_0.1_spmd.clone.sunk | while | flops 273155 | bytes 1203728 | solution.py:86
  37.8 1.3 constant_dynamic-slice_fusion.88
  111.5 9.1 %all_gather.54 = f32[4,3,2,128]{3,2,1,0:T(2,128)S(1)} all-gather(f32[1,3,2,128]{3,2,1,0:T(2,128)S(1)} %slice.734), channel_id=1, replica_groups=mesh['gx'=4,'gy'=8] {'gx'}, dimensions={0}, use_global_device_ids=true | all-gather | bytes 15360 | tf_op jit(solution)/shard_map/all_gather | solution.py:13
  121.4 6.6 %all_gather.55 = f32[4,3,2,128]{3,2,1,0:T(2,128)S(1)} all-gather(f32[1,3,2,128]{3,2,1,0:T(2,128)S(1)} %slice.735), channel_id=1, replica_groups=mesh['gx'=4,'gy'=8] {'gx'}, dimensions={0}, use_global_device_ids=true | all-gather | bytes 15360 | tf_op jit(solution)/shard_map/all_gather | solution.py:13
  128.6 8.7 %all_gather.56 = f32[4,3,2,128]{3,2,1,0:T(2,128)S(1)} all-gather(f32[1,3,2,128]{3,2,1,0:T(2,128)S(1)} %slice.736), channel_id=1, replica_groups=mesh['gx'=4,'gy'=8] {'gx'}, dimensions={0}, use_global_device_ids=true | all-gather | bytes 15360 | tf_op jit(solution)/shard_map/all_gather | solution.py:13
  138.0 6.6 %all_gather.57 = f32[4,3,2,128]{3,2,1,0:T(2,128)S(1)} all-gather(f32[1,3,2,128]{3,2,1,0:T(2,128)S(1)} %slice.737), channel_id=1, replica_groups=mesh['gx'=4,'gy'=8] {'gx'}, dimensions={0}, use_global_device_ids=true | all-gather | bytes 15360 | tf_op jit(solution)/shard_map/all_gather | solution.py:13
  145.3 8.7 %all_gather.58 = f32[4,3,2,128]{3,2,1,0:T(2,128)S(1)} all-gather(f32[1,3,2,128]{3,2,1,0:T(2,128)S(1)} %slice.738), channel_id=1, replica_groups=mesh['gx'=4,'gy'=8] {'gx'}, dimensions={0}, use_global_device_ids=true | all-gather | bytes 15360 | tf_op jit(solution)/shard_map/all_gather | solution.py:13
  154.7 6.6 %all_gather.59 = f32[4,3,2,128]{3,2,1,0:T(2,128)S(1)} all-gather(f32[1,3,2,128]{3,2,1,0:T(2,128)S(1)} %slice.739), channel_id=1, replica_groups=mesh['gx'=4,'gy'=8] {'gx'}, dimensions={0}, use_global_device_ids=true | all-gather | bytes 15360 | tf_op jit(solution)/shard_map/all_gather | solution.py:13
  162.0 8.7 %all_gather.60 = f32[4,3,2,128]{3,2,1,0:T(2,128)S(1)} all-gather(f32[1,3,2,128]{3,2,1,0:T(2,128)S(1)} %slice.740), channel_id=1, replica_groups=mesh['gx'=4,'gy'=8] {'gx'}, dimensions={0}, use_global_device_ids=true | all-gather | bytes 15360 | tf_op jit(solution)/shard_map/all_gather | solution.py:13
  170.7 2.5 add_divide_fusion.20
  173.9 5.5 %while.193 = (s32[]{:T(128)}, f32[3,2,128]{2,1,0:T(2,128)S(1)}, f32[3,2,128]{2,1,0:T(2,128)S(1)}, f32[16,8,3,2,128]{4,1,0,3,2:T(8,128)S(1)}, f32[16,8,3,2,128]{4...) while((s32[]{:T(128)}, f32[3,2,128]{2,1,0:T(2,128)S(1)}, ...), condition=%wide.region_5.6_spmd.clone, body=%wide.region_4.5_spmd.clone.sunk | while | flops 23817 | bytes 322916 | solution.py:111
  179.4 6.9 %all_gather.61 = f32[4,3,2,128]{3,2,1,0:T(2,128)S(1)} all-gather(f32[1,3,2,128]{3,2,1,0:T(2,128)S(1)} %bitcast.1391), channel_id=1, replica_groups=mesh['gx'=4,'gy'=8] {'gx'}, dimensions={0}, use_global_device_ids=true | all-gather | bytes 15360 | tf_op jit(solution)/shard_map/all_gather | solution.py:13
  186.3 8.7 %all_gather.62 = f32[4,3,2,128]{3,2,1,0:T(2,128)S(1)} all-gather(f32[1,3,2,128]{3,2,1,0:T(2,128)S(1)} %bitcast.1392), channel_id=1, replica_groups=mesh['gx'=4,'gy'=8] {'gx'}, dimensions={0}, use_global_device_ids=true | all-gather | bytes 15360 | tf_op jit(solution)/shard_map/all_gather | solution.py:13
  198.2 50.7 %while.194 = (s32[]{:T(128)}, f32[3,2,128]{2,1,0:T(2,128)S(1)}, f32[3,2,128]{2,1,0:T(2,128)S(1)}, f32[3,2,128]{2,1,0:T(2,128)S(1)}, f32[3,2,128]{2,1,0:T(2,128)S...) while((s32[]{:T(128)}, f32[3,2,128]{2,1,0:T(2,128)S(1)}, ...), condition=%wide.region_9.10_spmd.clone, body=%wide.region_8.9_spmd.clone.sunk | while | flops 273155 | bytes 1166780 | solution.py:86
  209.0 1.3 constant_dynamic-slice_fusion.89
  250.3 14.8 %all_gather.63 = f32[8,3,2,128]{3,2,1,0:T(2,128)S(1)} all-gather(f32[1,3,2,128]{3,2,1,0:T(2,128)S(1)} %slice.743), channel_id=1, replica_groups=mesh['gx'=4,'gy'=8] {'gy'}, dimensions={0}, use_global_device_ids=true | all-gather | bytes 27648 | tf_op jit(solution)/shard_map/all_gather | solution.py:13
  265.8 13.9 %all_gather.64 = f32[8,3,2,128]{3,2,1,0:T(2,128)S(1)} all-gather(f32[1,3,2,128]{3,2,1,0:T(2,128)S(1)} %slice.744), channel_id=1, replica_groups=mesh['gx'=4,'gy'=8] {'gy'}, dimensions={0}, use_global_device_ids=true | all-gather | bytes 27648 | tf_op jit(solution)/shard_map/all_gather | solution.py:13
  280.3 14.0 %all_gather.65 = f32[8,3,2,128]{3,2,1,0:T(2,128)S(1)} all-gather(f32[1,3,2,128]{3,2,1,0:T(2,128)S(1)} %slice.745), channel_id=1, replica_groups=mesh['gx'=4,'gy'=8] {'gy'}, dimensions={0}, use_global_device_ids=true | all-gather | bytes 27648 | tf_op jit(solution)/shard_map/all_gather | solution.py:13
  295.0 13.9 %all_gather.66 = f32[8,3,2,128]{3,2,1,0:T(2,128)S(1)} all-gather(f32[1,3,2,128]{3,2,1,0:T(2,128)S(1)} %slice.746), channel_id=1, replica_groups=mesh['gx'=4,'gy'=8] {'gy'}, dimensions={0}, use_global_device_ids=true | all-gather | bytes 27648 | tf_op jit(solution)/shard_map/all_gather | solution.py:13
  309.6 13.9 %all_gather.67 = f32[8,3,2,128]{3,2,1,0:T(2,128)S(1)} all-gather(f32[1,3,2,128]{3,2,1,0:T(2,128)S(1)} %slice.747), channel_id=1, replica_groups=mesh['gx'=4,'gy'=8] {'gy'}, dimensions={0}, use_global_device_ids=true | all-gather | bytes 27648 | tf_op jit(solution)/shard_map/all_gather | solution.py:13
  324.1 13.9 %all_gather.68 = f32[8,3,2,128]{3,2,1,0:T(2,128)S(1)} all-gather(f32[1,3,2,128]{3,2,1,0:T(2,128)S(1)} %slice.748), channel_id=1, replica_groups=mesh['gx'=4,'gy'=8] {'gy'}, dimensions={0}, use_global_device_ids=true | all-gather | bytes 27648 | tf_op jit(solution)/shard_map/all_gather | solution.py:13
  338.7 14.0 %all_gather.69 = f32[8,3,2,128]{3,2,1,0:T(2,128)S(1)} all-gather(f32[1,3,2,128]{3,2,1,0:T(2,128)S(1)} %slice.749), channel_id=1, replica_groups=mesh['gx'=4,'gy'=8] {'gy'}, dimensions={0}, use_global_device_ids=true | all-gather | bytes 27648 | tf_op jit(solution)/shard_map/all_gather | solution.py:13
  352.8 2.5 add_divide_fusion.18
  355.4 5.5 %while.195 = (s32[]{:T(128)}, f32[3,2,128]{2,1,0:T(2,128)S(1)}, f32[3,2,128]{2,1,0:T(2,128)S(1)}, f32[16,8,3,2,128]{4,1,0,3,2:T(8,128)S(1)}, f32[16,8,3,2,128]{4...) while((s32[]{:T(128)}, f32[3,2,128]{2,1,0:T(2,128)S(1)}, ...), condition=%wide.region_13.14_spmd.clone, body=%wide.region_12.13_spmd.clone.sunk | while | flops 23817 | bytes 322916 | solution.py:111
  360.9 13.9 %all_gather.70 = f32[8,3,2,128]{3,2,1,0:T(2,128)S(1)} all-gather(f32[1,3,2,128]{3,2,1,0:T(2,128)S(1)} %bitcast.1389), channel_id=1, replica_groups=mesh['gx'=4,'gy'=8] {'gy'}, dimensions={0}, use_global_device_ids=true | all-gather | bytes 27648 | tf_op jit(solution)/shard_map/all_gather | solution.py:13
  374.8 13.9 %all_gather.71 = f32[8,3,2,128]{3,2,1,0:T(2,128)S(1)} all-gather(f32[1,3,2,128]{3,2,1,0:T(2,128)S(1)} %bitcast.1390), channel_id=1, replica_groups=mesh['gx'=4,'gy'=8] {'gy'}, dimensions={0}, use_global_device_ids=true | all-gather | bytes 27648 | tf_op jit(solution)/shard_map/all_gather | solution.py:13
  (2191 shorter events, 161.7 us)
Async XLA Ops:
  0.0 11.2 %copy-start = (f32[3,2,128,128]{3,2,1,0:T(8,128)S(1)}, f32[3,2,128,128]{3,2,1,0:T(8,128)}, u32[]{:S(2)}) copy-start(f32[3,2,128,128]{3,2,1,0:T(8,128)} %param.18) | copy-start | bytes 1179652
  0.0 11.2 %copy-start.1 = (f32[2,128,128]{2,1,0:T(8,128)S(1)}, f32[2,128,128]{2,1,0:T(8,128)}, u32[]{:S(2)}) copy-start(f32[2,128,128]{2,1,0:T(8,128)} %param.19) | copy-start | bytes 393220
  0.9 6.1 %collective-permute-start = (f32[4,2,1,128]{3,2,1,0:T(1,128)S(1)}, f32[4,2,1,128]{3,2,1,0:T(1,128)S(1)}, u32[]{:S(2)}, u32[]{:S(2)}) collective-permute-start(f32[4,2,1,128]{3,2,1,0:T(1,128)S(1)} %get-tuple-element.1857), channel_id=1, source_target_pairs={{0,8},{8,16},{16,24},{1,9},{9,17},{17,25},{2,10},{10,18},{18,26},{... | collective-permute-start | bytes 12296 | tf_op jit(solution)/shard_map/ppermute | solution.py:30
  5.7 5.5 %collective-permute-start.1 = (f32[4,2,1,128]{3,2,1,0:T(1,128)S(1)}, f32[4,2,1,128]{3,2,1,0:T(1,128)S(1)}, u32[]{:S(2)}, u32[]{:S(2)}) collective-permute-start(f32[4,2,1,128]{3,2,1,0:T(1,128)S(1)} %get-tuple-element.1858), channel_id=1, source_target_pairs={{8,0},{16,8},{24,16},{9,1},{17,9},{25,17},{10,2},{18,10},{26,18},{... | collective-permute-start | bytes 12296 | tf_op jit(solution)/shard_map/ppermute | solution.py:33
  11.8 3.1 collective-permute-start.2
  13.4 4.9 %collective-permute-start.3 = (f32[4,2,130,1]{2,0,3,1:T(4,128)S(1)}, f32[4,2,130,1]{2,0,3,1:T(4,128)S(1)}, u32[]{:S(2)}, u32[]{:S(2)}) collective-permute-start(f32[4,2,130,1]{2,0,3,1:T(4,128)S(1)} %copy.66), channel_id=1, source_target_pairs={{1,0},{2,1},{3,2},{4,3},{5,4},{6,5},{7,6},{9,8},{10,9},{11,10},{12... | collective-permute-start | bytes 12488 | tf_op jit(solution)/shard_map/ppermute | solution.py:33
  23.6 0.7 copy-start.20
  29.3 0.7 copy-start.20
  35.1 0.7 copy-start.20
  40.8 0.7 copy-start.20
  46.3 0.7 copy-start.20
  52.0 0.7 copy-start.20
  96.4 0.7 copy-start.20
  110.1 0.7 copy-start.2
  110.1 10.6 %copy-start.4 = (f32[16,8,3,2,128]{4,3,2,1,0:T(2,128)}, f32[16,8,3,2,128]{4,3,2,1,0:T(2,128)S(1)}, u32[]{:S(2)}) copy-start(f32[16,8,3,2,128]{4,3,2,1,0:T(2,128)S(1)} %get-tuple-element.892) | copy-start | bytes 1179652
  110.1 17.8 %copy-start.5 = (f32[16,8,3,2,128]{4,3,2,1,0:T(2,128)}, f32[16,8,3,2,128]{4,3,2,1,0:T(2,128)S(1)}, u32[]{:S(2)}) copy-start(f32[16,8,3,2,128]{4,3,2,1,0:T(2,128)S(1)} %get-tuple-element.893) | copy-start | bytes 1179652
  110.1 27.2 %copy-start.6 = (f32[16,8,3,2,128]{4,3,2,1,0:T(2,128)}, f32[16,8,3,2,128]{4,3,2,1,0:T(2,128)S(1)}, u32[]{:S(2)}) copy-start(f32[16,8,3,2,128]{4,3,2,1,0:T(2,128)S(1)} %get-tuple-element.894) | copy-start | bytes 1179652
  110.2 34.5 %copy-start.8 = (f32[16,8,3,2,128]{4,3,2,1,0:T(2,128)}, f32[16,8,3,2,128]{4,3,2,1,0:T(2,128)S(1)}, u32[]{:S(2)}) copy-start(f32[16,8,3,2,128]{4,3,2,1,0:T(2,128)S(1)} %get-tuple-element.895) | copy-start | bytes 1179652
  110.2 43.8 %copy-start.9 = (f32[16,8,3,2,128]{4,3,2,1,0:T(2,128)}, f32[16,8,3,2,128]{4,3,2,1,0:T(2,128)S(1)}, u32[]{:S(2)}) copy-start(f32[16,8,3,2,128]{4,3,2,1,0:T(2,128)S(1)} %get-tuple-element.896) | copy-start | bytes 1179652
  110.2 51.1 %copy-start.7 = (f32[16,8,3,2,128]{4,3,2,1,0:T(2,128)}, f32[16,8,3,2,128]{4,3,2,1,0:T(2,128)S(1)}, u32[]{:S(2)}) copy-start(f32[16,8,3,2,128]{4,3,2,1,0:T(2,128)S(1)} %get-tuple-element.897) | copy-start | bytes 1179652
  111.5 59.2 %copy-start.3 = (f32[16,8,3,2,128]{4,3,2,1,0:T(2,128)S(1)}, f32[16,8,3,2,128]{4,3,2,1,0:T(2,128)}, u32[]{:S(2)}) copy-start(f32[16,8,3,2,128]{4,3,2,1,0:T(2,128)} %copy-done.2) | copy-start | bytes 1179652
  173.3 0.7 copy-start.19
  197.5 0.7 copy-start.18
  197.5 0.7 copy-start.22
  248.9 0.7 copy-start.10
  248.9 16.2 %copy-start.12 = (f32[16,8,3,2,128]{4,3,2,1,0:T(2,128)}, f32[16,8,3,2,128]{4,3,2,1,0:T(2,128)S(1)}, u32[]{:S(2)}) copy-start(f32[16,8,3,2,128]{4,3,2,1,0:T(2,128)S(1)} %get-tuple-element.908) | copy-start | bytes 1179652
  248.9 30.7 %copy-start.13 = (f32[16,8,3,2,128]{4,3,2,1,0:T(2,128)}, f32[16,8,3,2,128]{4,3,2,1,0:T(2,128)S(1)}, u32[]{:S(2)}) copy-start(f32[16,8,3,2,128]{4,3,2,1,0:T(2,128)S(1)} %get-tuple-element.909) | copy-start | bytes 1179652
  248.9 45.4 %copy-start.14 = (f32[16,8,3,2,128]{4,3,2,1,0:T(2,128)}, f32[16,8,3,2,128]{4,3,2,1,0:T(2,128)S(1)}, u32[]{:S(2)}) copy-start(f32[16,8,3,2,128]{4,3,2,1,0:T(2,128)S(1)} %get-tuple-element.910) | copy-start | bytes 1179652
  249.0 59.9 %copy-start.16 = (f32[16,8,3,2,128]{4,3,2,1,0:T(2,128)}, f32[16,8,3,2,128]{4,3,2,1,0:T(2,128)S(1)}, u32[]{:S(2)}) copy-start(f32[16,8,3,2,128]{4,3,2,1,0:T(2,128)S(1)} %get-tuple-element.911) | copy-start | bytes 1179652
  249.0 74.5 %copy-start.17 = (f32[16,8,3,2,128]{4,3,2,1,0:T(2,128)}, f32[16,8,3,2,128]{4,3,2,1,0:T(2,128)S(1)}, u32[]{:S(2)}) copy-start(f32[16,8,3,2,128]{4,3,2,1,0:T(2,128)S(1)} %get-tuple-element.912) | copy-start | bytes 1179652
  249.0 89.0 %copy-start.15 = (f32[16,8,3,2,128]{4,3,2,1,0:T(2,128)}, f32[16,8,3,2,128]{4,3,2,1,0:T(2,128)S(1)}, u32[]{:S(2)}) copy-start(f32[16,8,3,2,128]{4,3,2,1,0:T(2,128)S(1)} %get-tuple-element.913) | copy-start | bytes 1179652
  280.3 72.5 %copy-start.11 = (f32[16,8,3,2,128]{4,3,2,1,0:T(2,128)S(1)}, f32[16,8,3,2,128]{4,3,2,1,0:T(2,128)}, u32[]{:S(2)}) copy-start(f32[16,8,3,2,128]{4,3,2,1,0:T(2,128)} %copy-done.10) | copy-start | bytes 1179652
  (41 other events, 27.2 us)
where the time goes:
time: 396 us; the launch traced here: 390 us
  blocking collectives  197 us (50%)
  local copies, waits for them, and re-layouts  119 us (30%)
  other arithmetic  49.3 us (12%)
  starting transfers between devices  8.71 us (2%)
  loops' own time  7.83 us (2%)
  waiting for transfers between devices  7.31 us (2%)
    all_gather x18, blocking collectives, prefix_2(): gathered = jax.tree.map(lambda a: lax.all_gather(a, axis), part)  197 us
    slice x96, local copies, waits for them, and re-layouts, forward(): lax.scan(advance, neutral_of(source.shape[1:]), (lower_face, upper_face,...  69.3 us
    while x416, other arithmetic  30.8 us
    while x1056, local copies, waits for them, and re-layouts  28.8 us
    concatenate x32, other arithmetic, forward(): lax.scan(advance, neutral_of(source.shape[1:]), (lower_face, upper_face,...  10.1 us
  transfers between devices with their start and end apart: 4, of which 2 were waited for; matrix products, arithmetic and copies ran while one was open for 0% of the time, Pallas kernels for 0%

commit v1 on v0

v1 whole, which is shorter than its diff:
```python
import functools

import jax
import jax.numpy as jnp
from jax import lax
from jax.experimental import pallas as pl
from jax.experimental.pallas import tpu as pltpu
from jax.sharding import PartitionSpec as P

courant = 0.25
SUB = 8
MESH = pl.DeviceIdType.MESH


def halves(a):
    a = a.reshape((a.shape[0] // 2, 2) + a.shape[1:])
    return a[:, 0], a[:, 1]


def plus(a, b):
    return b if a is None else (a if b is None else a + b)


def join_matrix(c1, c2, gr1, gl2, gl1, gr2):
    g = plus(gr1, gl2)
    r = 1.0 / (c1 + c2 + g)
    p, q = c1 * r, c2 * r
    return (p, q, r), p * c2, plus(gl1, p * g), gr2 + q * g


def tree_matrix(c, gl, gr):
    levels = []
    while c.shape[0] > 1:
        c1, c2 = halves(c)
        gr1, gr2 = halves(gr)
        gl1, gl2 = (None, None) if gl is None else halves(gl)
        level, c, gl, gr = join_matrix(c1, c2, gr1, gl2, gl1, gr2)
        levels.append(level)
    return levels, c[0], gl[0], gr[0]


def tree_source(il, ir, levels, widen):
    mids = []
    for level in levels:
        p, q, r = (widen(a) for a in level)
        ir1, ir2 = halves(ir)
        il1, il2 = (None, None) if il is None else halves(il)
        i = plus(ir1, il2)
        mids.append(i * r)
        il = plus(il1, p * i)
        ir = ir2 + q * i
    return mids, il[0], ir[0]


def tree_down(left, right, levels, mids, widen):
    w = right[None]
    for level, mid in zip(reversed(levels), reversed(mids)):
        p, q = widen(level[0]), widen(level[1])
        wl = left[None] if w.shape[0] == 1 else jnp.concatenate([left[None], w[:-1]], 0)
        m = mid + p * wl + q * w
        w = jnp.stack([m, w], 1).reshape((2 * w.shape[0],) + w.shape[1:])
    return w


def roll_rows(a, shift):
    flat = a.reshape((-1,) + a.shape[-2:])
    out = [pltpu.roll(flat[k], shift % SUB, 0) for k in range(flat.shape[0])]
    return jnp.stack(out).reshape(a.shape)


def rows_matrix(c, gl, gr):
    levels = []
    for shift in (1, 2, 4):
        level, c, gl, gr = join_matrix(
            roll_rows(c, shift), c, roll_rows(gr, shift), gl, roll_rows(gl, shift), gr
        )
        levels.append(level)
    return levels, c, gl, gr


def rows_source(il, ir, levels):
    mids = []
    for shift, (p, q, r) in zip((1, 2, 4), levels):
        i = roll_rows(ir, shift) + il
        mids.append(i * r)
        il = roll_rows(il, shift) + p * i
        ir = ir + q * i
    return mids, il, ir


def rows_down(left, right, levels, mids, row):
    def solve(k, wl, wr):
        return mids[k] + levels[k][0] * wl + levels[k][1] * wr

    m = solve(2, left, right)
    m3 = jnp.broadcast_to(m[..., 7:8, :], m.shape)
    wr = jnp.where(row < 4, m3, right)
    m = solve(1, jnp.where(row < 4, left, m3), wr)
    m1 = jnp.broadcast_to(m[..., 3:4, :], m.shape)
    m5 = jnp.broadcast_to(m[..., 7:8, :], m.shape)
    wl = jnp.where(row < 2, left, jnp.where(row < 4, m1, jnp.where(row < 6, m3, m5)))
    wr = jnp.where(row < 2, m1, jnp.where(row < 4, m3, jnp.where(row < 6, m5, right)))
    m = solve(0, wl, wr)
    w = jnp.where(row % 2 == 1, wr, roll_rows(m, 7))
    return jnp.where(row == 0, left, roll_rows(w, 1)), w


def spread(tile, first):
    row = lax.broadcasted_iota(jnp.int32, tile.shape, 1)
    return jnp.where(row % 2 == 0, tile[:, first : first + 1], tile[:, first + 1 : first + 2])


def kernel(
    dx, dy, vel, dif, out,
    xh_send, xh_recv, yh_send, yh_recv, xg, ym, yr, wx, wy, scr, scr_d,
    hs, hr, xs, xr, yms, ymr, yrs, yrr,
):
    ncomp, planes, nx, ny = vel.shape
    tx, ty = nx // SUB, ny // SUB
    nf = ncomp * planes
    ix, iy = lax.axis_index("gx"), lax.axis_index("gy")
    x_peers = [lax.rem(ix + o, dx) for o in range(1, dx)]
    y_peers = [lax.rem(iy + o, dy) for o in range(1, dy)]

    barrier = pltpu.get_barrier_semaphore()
    for peer in x_peers:
        pl.semaphore_signal(barrier, inc=1, device_id={"gx": peer}, device_id_type=MESH)
    for peer in y_peers:
        pl.semaphore_signal(barrier, inc=1, device_id={"gy": peer}, device_id_type=MESH)

    def copy(src, dst, send, recv, where):
        return pltpu.make_async_remote_copy(
            src_ref=src, dst_ref=dst, send_sem=send, recv_sem=recv,
            device_id=where, device_id_type=MESH,
        )

    def wide(a):
        return a[:, None]

    row = lax.broadcasted_iota(jnp.int32, (SUB, ny), 0)
    row_y = lax.broadcasted_iota(jnp.int32, (SUB, nx), 0)
    lane = lax.broadcasted_iota(jnp.int32, (nx, ny), 1)

    v = jnp.stack([vel[:, :, pl.ds(t, SUB, stride=tx), :] for t in range(tx)])
    d = jnp.stack([dif[:, pl.ds(t, SUB, stride=tx), :] for t in range(tx)])
    fields = [v[:, c, p].reshape(nx, ny) for c in range(ncomp) for p in range(planes)]
    fields += [d[:, p].reshape(nx, ny) for p in range(planes)]

    for f in range(nf + planes):
        ref = vel.at[f // planes, f % planes] if f < nf else dif.at[f - nf]
        xh_send[0, f : f + 1, :] = ref[nx - 1 : nx, :]
        xh_send[1, f : f + 1, :] = ref[0:1, :]
    edges = jnp.zeros((nx, ny), jnp.float32)
    for f, a in enumerate(fields):
        edges = jnp.where(lane // 2 == f, pltpu.roll(a, 2 * f + 1, 1), edges)
    yh_send[...] = edges.T[: 2 * SUB]

    x_high, x_low = {"gx": lax.rem(ix + 1, dx)}, {"gx": lax.rem(ix + dx - 1, dx)}
    y_high, y_low = {"gy": lax.rem(iy + 1, dy)}, {"gy": lax.rem(iy + dy - 1, dy)}
    halos = [
        (copy(xh_send.at[0], xh_recv.at[0], hs.at[0], hr.at[0], x_high), ix < dx - 1, ix > 0),
        (copy(xh_send.at[1], xh_recv.at[1], hs.at[1], hr.at[1], x_low), ix > 0, ix < dx - 1),
        (copy(yh_send, yh_recv.at[0], hs.at[2], hr.at[2], y_high), iy < dy - 1, iy > 0),
        (copy(yh_send, yh_recv.at[1], hs.at[3], hr.at[3], y_low), iy > 0, iy < dy - 1),
    ]
    pl.semaphore_wait(barrier, dx + dy - 2)
    for c, sends, takes in halos:
        pl.when(sends)(c.start)
    for c, sends, takes in halos:
        pl.when(takes)(c.wait_recv)

    def low_row(f):
        return jnp.where(ix > 0, xh_recv[0, f : f + 1, :], 0.0)

    def high_row(f):
        return jnp.where(ix < dx - 1, xh_recv[1, f : f + 1, :], 0.0)

    first = [jnp.where(row == 0, low_row(nf + p), pltpu.roll(d[tx - 1, p], 1, 0)) for p in range(planes)]
    ax = 0.5 * (jnp.concatenate([jnp.stack(first)[None], d[:-1]], 0) + d)
    end = (row == SUB - 1) & (ix == dx - 1)
    gr = jnp.concatenate([jnp.ones_like(d[:-1]), (1.0 + jnp.where(end, 0.5 * d[tx - 1], 0.0))[None]], 0)
    xt, c, gl, gr = tree_matrix(ax, None, gr)
    xrow, c, gl, gr = rows_matrix(c, gl, gr)
    for p in range(planes):
        xg[ix, p : p + 1, :] = c[p, 7:8]
        xg[ix, planes + p : planes + p + 1, :] = gl[p, 7:8]
        xg[ix, 2 * planes + p : 2 * planes + p + 1, :] = gr[p, 7:8]

    take = lax.broadcasted_iota(jnp.int32, (2 * SUB, nx), 0) % 2 == 0
    halo = jnp.where(
        take, jnp.where(iy > 0, yh_recv[0], 0.0), jnp.where(iy < dy - 1, yh_recv[1], 0.0)
    )
    halo = jnp.concatenate([halo, jnp.zeros((ny - 2 * SUB, nx), jnp.float32)], 0).T

    def before_y(f):
        h = pltpu.roll(halo, ny - 2 * f - 1, 1)
        return h, pltpu.roll(jnp.where(lane == ny - 1, h, fields[f]), 1, 1)

    source = []
    for cc in range(ncomp):
        for p in range(planes):
            f = cc * planes + p
            a = v[:, cc, p]
            lo = jnp.where(row == 0, low_row(f), pltpu.roll(a[tx - 1], 1, 0))
            hi = jnp.where(row == SUB - 1, high_row(f), pltpu.roll(a[0], SUB - 1, 0))
            grad_x = jnp.concatenate([a[1:], hi[None]], 0) - jnp.concatenate([lo[None], a[:-1]], 0)
            h, prev = before_y(f)
            grad_y = pltpu.roll(jnp.where(lane == 0, h, fields[f]), ny - 1, 1) - prev
            grad_y = grad_y.reshape(tx, SUB, ny)
            source.append(a - (0.5 * courant) * (v[:, 0, p] * grad_x + v[:, 1, p] * grad_y))
    source = jnp.stack(source, 1).reshape(v.shape)
    xmids, il, ir = tree_source(None, source, xt, wide)
    xrowmids, il, ir = rows_source(il, ir, xrow)
    for f in range(nf):
        xg[ix, SUB + f : SUB + f + 1, :] = il[f // planes, f % planes, 7:8]
        xg[ix, 2 * SUB + f : 2 * SUB + f + 1, :] = ir[f // planes, f % planes, 7:8]
    x_copies = [
        copy(xg.at[ix], xg.at[ix], xs.at[o], xr.at[o], {"gx": peer})
        for o, peer in enumerate(x_peers)
    ]
    for c in x_copies:
        c.start()

    for p in range(planes):
        scr_d[p] = (0.5 * (before_y(nf + p)[1] + fields[nf + p])).T
    ay = jnp.stack([scr_d[:, pl.ds(t, SUB, stride=ty), :] for t in range(ty)])
    end = (row_y == SUB - 1) & (iy == dy - 1)
    last = [
        1.0 + jnp.where(end, 0.5 * yh_send[2 * (nf + p) : 2 * (nf + p) + 1, :], 0.0)
        for p in range(planes)
    ]
    gr = jnp.concatenate([jnp.ones_like(ay[:-1]), jnp.stack(last)[None]], 0)
    yt, c, gl, gr = tree_matrix(ay, None, gr)
    yrow, c, gl, gr = rows_matrix(c, gl, gr)
    for p in range(planes):
        ym[iy, p : p + 1, :] = c[p, 7:8]
        ym[iy, planes + p : planes + p + 1, :] = gl[p, 7:8]
        ym[iy, 2 * planes + p : 2 * planes + p + 1, :] = gr[p, 7:8]
    ym_copies = [
        copy(ym.at[iy], ym.at[iy], yms.at[o], ymr.at[o], {"gy": peer})
        for o, peer in enumerate(y_peers)
    ]
    for c in ym_copies:
        c.start()

    def same(a):
        return a

    def ends_matrix(tile):
        c, gl, gr = (spread(tile, k * planes) for k in range(3))
        levels, c, gl, gr = tree_matrix(c, gl, gr)
        return levels, 1.0 / (c + gr)

    def ends_solve(il, ir, levels, inverse, held, place):
        mids, il, ir = tree_source(il, ir, levels, same)
        held[0] = jnp.zeros(held.shape[1:], jnp.float32)
        held[1:] = tree_down(jnp.zeros_like(ir), ir * inverse, levels, mids, same)
        low, high = held[place], held[place + 1]

        def split(a):
            parts = [jnp.broadcast_to(a[f : f + 1], a.shape) for f in range(nf)]
            return jnp.stack(parts).reshape((ncomp, planes) + a.shape)

        return split(low), split(high)

    for c in x_copies:
        c.wait_recv()
    levels, inverse = ends_matrix(xg[:, :SUB])
    low, high = ends_solve(xg[:, SUB : 2 * SUB], xg[:, 2 * SUB :], levels, inverse, wx, ix)
    left, right = rows_down(low, high, xrow, xrowmids, row)
    middle = tree_down(left, right, xt, xmids, wide)

    for f in range(nf):
        cc, p = f // planes, f % planes
        scr[cc, p] = middle[:, cc, p].reshape(nx, ny).T
    m = jnp.stack([scr[:, :, pl.ds(t, SUB, stride=ty), :] for t in range(ty)])
    ymids, il, ir = tree_source(None, m, yt, wide)
    yrowmids, il, ir = rows_source(il, ir, yrow)
    for f in range(nf):
        yr[iy, f : f + 1, :] = il[f // planes, f % planes, 7:8]
        yr[iy, SUB + f : SUB + f + 1, :] = ir[f // planes, f % planes, 7:8]
    yr_copies = [
        copy(yr.at[iy], yr.at[iy], yrs.at[o], yrr.at[o], {"gy": peer})
        for o, peer in enumerate(y_peers)
    ]
    for c in yr_copies:
        c.start()

    for c in ym_copies:
        c.wait_recv()
    levels, inverse = ends_matrix(ym[...])
    for c in yr_copies:
        c.wait_recv()
    low, high = ends_solve(yr[:, :SUB], yr[:, SUB:], levels, inverse, wy, iy)
    left, right = rows_down(low, high, yrow, yrowmids, row_y)
    w = tree_down(left, right, yt, ymids, wide)
    for t in range(ty):
        scr[:, :, pl.ds(t, SUB, stride=ty), :] = w[t]
    for f in range(nf):
        cc, p = f // planes, f % planes
        a = scr[cc, p].T.reshape(tx, SUB, ny)
        for t in range(tx):
            out[cc, p, pl.ds(t, SUB, stride=tx), :] = a[t]

    for c, sends, takes in halos:
        pl.when(sends)(c.wait_send)
    for c in x_copies + ym_copies + yr_copies:
        c.wait_send()


def local(dx, dy, velocity, diffusion):
    ncomp, planes, nx, ny = velocity.shape
    vmem = pl.BlockSpec(memory_space=pltpu.VMEM)
    f32 = jnp.float32
    dma = pltpu.SemaphoreType.DMA
    return pl.pallas_call(
        functools.partial(kernel, dx, dy),
        out_shape=jax.ShapeDtypeStruct(velocity.shape, f32),
        in_specs=[vmem, vmem],
        out_specs=vmem,
        scratch_shapes=[
            pltpu.VMEM((2, SUB, ny), f32),
            pltpu.VMEM((2, SUB, ny), f32),
            pltpu.VMEM((2 * SUB, nx), f32),
            pltpu.VMEM((2, 2 * SUB, nx), f32),
            pltpu.VMEM((dx, 3 * SUB, ny), f32),
            pltpu.VMEM((dy, SUB, nx), f32),
            pltpu.VMEM((dy, 2 * SUB, nx), f32),
            pltpu.VMEM((dx + 1, SUB, ny), f32),
            pltpu.VMEM((dy + 1, SUB, nx), f32),
            pltpu.VMEM((ncomp, planes, ny, nx), f32),
            pltpu.VMEM((planes, ny, nx), f32),
            dma((4,)), dma((4,)),
            dma((dx,)), dma((dx,)),
            dma((dy,)), dma((dy,)),
            dma((dy,)), dma((dy,)),
        ],
        compiler_params=pltpu.CompilerParams(
            collective_id=0, has_side_effects=True, vmem_limit_bytes=48 * 1024 * 1024
        ),
    )(velocity, diffusion)


def solution(mesh):
    in_specs = (P(None, None, "gx", "gy"), P(None, "gx", "gy"))
    out_specs = P(None, None, "gx", "gy")
    body = functools.partial(local, mesh.shape["gx"], mesh.shape["gy"])
    return jax.shard_map(body, mesh=mesh, in_specs=in_specs, out_specs=out_specs, check_vma=False)
```

time: 396 us -> 19.2 us (0.05); the launches traced: 390 us -> 19 us
  blocking collectives: 197 us -> 0 us
  local copies, waits for them, and re-layouts: 119 us -> 2.65 us
  other arithmetic: 49.3 us -> 0 us
  Pallas kernels: 0 us -> 16.4 us
  starting transfers between devices: 8.71 us -> 0 us
  loops' own time: 7.83 us -> 0 us
  waiting for transfers between devices: 7.31 us -> 0 us
    all_gather x18 -> x0, blocking collectives: 197 us -> none  [prefix_2(): gathered = jax.tree.map(lambda a: lax.all_gather(a, axis), part)]
    slice x117 -> x0, local copies, waits for them, and re-layouts: 79.7 us -> none  [the longest x96 69.3 us: forward(): lax.scan(advance, neutral_of(source.shape[1:]), (lower_face, upper_face,...]
    while x416 -> x0, other arithmetic: 30.8 us -> none
    while x1056 -> x0, local copies, waits for them, and re-layouts: 28.8 us -> none
    pallas_call x0 -> x1, Pallas kernels: none -> 16.4 us  [local(): pl.pallas_call(functools.partial(kernel, dx, dy), out_shape=jax.ShapeDtyp...]
    concatenate x33 -> x0, other arithmetic: 10.2 us -> none  [the longest x32 10.1 us: forward(): lax.scan(advance, neutral_of(source.shape[1:]), (lower_face, upper_face,...]
    ppermute x4 -> x0, starting transfers between devices: 8.71 us -> none  [the longest x2 6.12 us: padded_2(): lax.ppermute(lax.slice_in_dim(block, block.shape[dim] - width, None, axis...]
    another operation x8 -> x0, loops' own time: 7.83 us -> none  [the longest x2 4.95 us: forward(): lax.scan(advance, neutral_of(source.shape[1:]), (lower_face, upper_face,...]
  transfers between devices with their start and end apart: 4 -> 0, of which waited for: 2 -> 0; matrix products, arithmetic and copies ran while one was open for 0% -> 0% of each run, Pallas kernels for 0% -> 0%
where the time goes in v1:
time: 19.2 us; the launch traced here: 19 us
  Pallas kernels  16.4 us (85%)
  local copies, waits for them, and re-layouts  2.65 us (14%)
    pallas_call x1, Pallas kernels, local(): pl.pallas_call(functools.partial(kernel, dx, dy), out_shape=jax.ShapeDtyp...  16.4 us
    unnamed x5, local copies, waits for them, and re-layouts  2.65 us

profile of v1, /device:TPU:0, one launch (start us, length us, event | category | flops | bytes accessed | tf_op | source)
XLA Modules:
  0.0 19.0 jit_solution(9949407024756581585)
XLA Ops:
  0.0 0.0 copy-start
  0.0 1.0 %copy-done = f32[3,2,128,128]{3,2,1,0:T(8,128)S(1)} copy-done((f32[3,2,128,128]{3,2,1,0:T(8,128)S(1)}, f32[3,2,128,128]{3,2,1,0:T(8,128)}, u32[]{:S(2)}) %copy-start) | copy-done | bytes 393240
  1.0 0.0 copy-start.1
  1.0 0.9 %copy-done.1 = f32[2,128,128]{2,1,0:T(8,128)S(1)} copy-done((f32[2,128,128]{2,1,0:T(8,128)S(1)}, f32[2,128,128]{2,1,0:T(8,128)}, u32[]{:S(2)}) %copy-start.1) | copy-done | bytes 131096
  1.9 16.4 %shard_map.28 = f32[3,2,128,128]{3,2,1,0:T(8,128)S(1)} custom-call(f32[3,2,128,128]{3,2,1,0:T(8,128)S(1)} %copy-done, f32[2,128,128]{2,1,0:T(8,128)S(1)} %copy-done.1), custom_call_target="tpu_custom_call" | custom-call | tf_op jit(solution)/shard_map/pallas_call | solution.py:316
  18.3 0.7 %copy.4 = f32[3,2,128,128]{3,2,1,0:T(8,128)} copy(f32[3,2,128,128]{3,2,1,0:T(8,128)S(1)} %shard_map.28) | data formatting | bytes 786432
Async XLA Ops:
  0.0 1.0 %copy-start = (f32[3,2,128,128]{3,2,1,0:T(8,128)S(1)}, f32[3,2,128,128]{3,2,1,0:T(8,128)}, u32[]{:S(2)}) copy-start(f32[3,2,128,128]{3,2,1,0:T(8,128)} %vel.1) | copy-start | bytes 1179652
  1.0 0.9 %copy-start.1 = (f32[2,128,128]{2,1,0:T(8,128)S(1)}, f32[2,128,128]{2,1,0:T(8,128)}, u32[]{:S(2)}) copy-start(f32[2,128,128]{2,1,0:T(8,128)} %dif.1) | copy-start | bytes 393220

commit v2 on v1

v2 whole, which is shorter than its diff:
```python
import functools

import jax
import jax.numpy as jnp
from jax import lax
from jax.experimental import pallas as pl
from jax.experimental.pallas import tpu as pltpu
from jax.sharding import PartitionSpec as P

courant = 0.25
SUB = 8
MESH = pl.DeviceIdType.MESH


def halves(a):
    a = a.reshape((a.shape[0] // 2, 2) + a.shape[1:])
    return a[:, 0], a[:, 1]


def plus(a, b):
    return b if a is None else (a if b is None else a + b)


def join_matrix(c1, c2, gr1, gl2, gl1, gr2):
    g = gr1 + gl2
    r = 1.0 / (c1 + c2 + g)
    p, q = c1 * r, c2 * r
    return (p, q, r), p * c2, gl1 + p * g, gr2 + q * g


def tree_matrix(d, row):
    prev = jnp.concatenate([roll_rows(d[-1:], 1), d[:-1]], 0)
    c = 0.5 * (prev + d)
    kept = row == 0
    c1, c2 = halves(c)
    r = 1.0 / (c1 + c2 + 1.0)
    p, q = c1 * r, c2 * r
    p, q, r = (
        jnp.concatenate([jnp.where(kept, value, a[:1]), a[1:]], 0)
        for a, value in ((p, 1.0), (q, 0.0), (r, 0.0))
    )
    levels = [(p, q, r)]
    c, gl, gr = p * c2, p, 1.0 + q
    while c.shape[0] > 1:
        c1, c2 = halves(c)
        gr1, gr2 = halves(gr)
        gl1, gl2 = halves(gl)
        level, c, gl, gr = join_matrix(c1, c2, gr1, gl2, gl1, gr2)
        levels.append(level)
    return levels, c[0], gl[0], gr[0]


def tree_source(il, ir, levels, widen):
    mids = []
    for level in levels:
        p, q, r = (widen(a) for a in level)
        ir1, ir2 = halves(ir)
        il1, il2 = (None, None) if il is None else halves(il)
        i = plus(ir1, il2)
        mids.append(i * r)
        il = plus(il1, p * i)
        ir = ir2 + q * i
    return mids, il[0], ir[0]


def tree_down(left, right, levels, mids, widen):
    w = right[None]
    for level, mid in zip(reversed(levels), reversed(mids)):
        p, q = widen(level[0]), widen(level[1])
        wl = left[None] if w.shape[0] == 1 else jnp.concatenate([left[None], w[:-1]], 0)
        m = mid + p * wl + q * w
        w = jnp.stack([m, w], 1).reshape((2 * w.shape[0],) + w.shape[1:])
    return w


def roll_rows(a, shift):
    flat = a.reshape((-1,) + a.shape[-2:])
    out = [pltpu.roll(flat[k], shift % SUB, 0) for k in range(flat.shape[0])]
    return jnp.stack(out).reshape(a.shape)


def rows_matrix(c, gl, gr):
    levels = []
    for shift in (1, 2, 4):
        level, c, gl, gr = join_matrix(
            roll_rows(c, shift), c, roll_rows(gr, shift), gl, roll_rows(gl, shift), gr
        )
        levels.append(level)
    return levels, c, gl, gr


def rows_source(il, ir, levels):
    mids = []
    for shift, (p, q, r) in zip((1, 2, 4), levels):
        i = roll_rows(ir, shift) + il
        mids.append(i * r)
        il = roll_rows(il, shift) + p * i
        ir = ir + q * i
    return mids, il, ir


def rows_down(left, right, levels, mids, row):
    def solve(k, wl, wr):
        return mids[k] + levels[k][0] * wl + levels[k][1] * wr

    m = solve(2, left, right)
    m3 = jnp.broadcast_to(m[..., 7:8, :], m.shape)
    wr = jnp.where(row < 4, m3, right)
    m = solve(1, jnp.where(row < 4, left, m3), wr)
    m1 = jnp.broadcast_to(m[..., 3:4, :], m.shape)
    m5 = jnp.broadcast_to(m[..., 7:8, :], m.shape)
    wl = jnp.where(row < 2, left, jnp.where(row < 4, m1, jnp.where(row < 6, m3, m5)))
    wr = jnp.where(row < 2, m1, jnp.where(row < 4, m3, jnp.where(row < 6, m5, right)))
    m = solve(0, wl, wr)
    w = jnp.where(row % 2 == 1, wr, roll_rows(m, 7))
    return jnp.where(row == 0, left, roll_rows(w, 1)), w


def pick(place, items):
    out = items[0]
    for k in range(1, len(items)):
        out = jnp.where(place == k, items[k], out)
    return out


def tile_of(a, row):
    flat = a.reshape((-1,) + a.shape[-2:])
    out = jnp.zeros_like(flat[0])
    for f in range(flat.shape[0]):
        out = jnp.where(row == f, pltpu.roll(flat[f], (f + 1) % SUB, 0), out)
    return out


def put_matrix(ref, place, c, gl, gr, first, last):
    planes = c.shape[0]
    for p in range(planes):
        ref[place, p : p + 1, :] = c[p, SUB - 1 :]
        ref[place, planes + p : planes + p + 1, :] = gl[p, SUB - 1 :]
        ref[place, 2 * planes + p : 2 * planes + p + 1, :] = gr[p, SUB - 1 :]
        ref[place, 3 * planes + p : 3 * planes + p + 1, :] = first[p]
        ref[place, 4 * planes + p : 4 * planes + p + 1, :] = last[p]


def ends_matrix(ref, count, place, planes, row):
    def spread(k, quantity):
        return pick(
            row % planes,
            [ref[k, quantity * planes + p : quantity * planes + p + 1, :] for p in range(planes)],
        )

    c, gl, gr, first, last = ([spread(k, j) for k in range(count)] for j in range(5))
    link = [0.5 * (last[k - 1] + first[k]) if k else 0.5 * first[0] for k in range(count)]
    left, t_first, t_last = [gl[0] + link[0]], [], []
    right, u_first, u_last = [gr[-1] + 0.5 * last[-1]], [], []
    for k in range(count):
        t_first.append(c[k] / (c[k] + left[k]))
        g = gr[k] + t_first[k] * left[k]
        j = count - 1 - k
        u_last.insert(0, c[j] / (c[j] + right[0]))
        h = gl[j] + u_last[0] * right[0]
        if k < count - 1:
            t_last.append(link[k + 1] / (link[k + 1] + g))
            left.append(gl[k + 1] + t_last[k] * g)
            u_first.insert(0, link[j] / (link[j] + h))
            right.insert(0, gr[j - 1] + u_first[0] * h)
    u_first.insert(0, None)
    own_c, g, h = pick(place, c), pick(place, left), pick(place, right)
    r = 1.0 / (own_c * (g + h) + g * h)
    inner = ((own_c + h) * r, own_c * r, (own_c + g) * r)
    t_own, u_own = pick(place, t_first), pick(place, u_last)
    zero = jnp.zeros_like(own_c)
    from_first, from_last = [zero] * count, [zero] * count
    x = None
    for e in range(1, count):
        through = zero if x is None else x * t_first[e - 1] * t_last[e - 1]
        x = jnp.where(place == e - 1, t_last[e - 1], through)
        from_last[e], from_first[e] = x, x * t_own
    y = None
    for e in range(count - 2, -1, -1):
        through = zero if y is None else y * u_last[e + 1] * u_first[e + 1]
        y = jnp.where(place == e + 1, u_first[e + 1], through)
        from_first[e] = jnp.where(place > e, y, from_first[e])
        from_last[e] = jnp.where(place > e, y * u_own, from_last[e])
    return from_first, from_last, inner


def ends_send(send, il, ir, from_first, from_last, copies):
    for e in range(len(from_first)):
        send[e] = il * from_first[e] + ir * from_last[e]
    for c in copies:
        c.start()


def ends_solve(recv, il, ir, inner, count, place, ncomp, planes):
    for k in range(count):
        tile = recv[k]
        il = il + jnp.where(k < place, tile, 0.0)
        ir = ir + jnp.where(k > place, tile, 0.0)
    low = inner[0] * il + inner[1] * ir
    high = inner[1] * il + inner[2] * ir

    def split(a):
        parts = [jnp.broadcast_to(a[f : f + 1], a.shape) for f in range(ncomp * planes)]
        return jnp.stack(parts).reshape((ncomp, planes) + a.shape)

    return split(low), split(high)


def kernel(
    dx, dy, vel_in, dif_in, out,
    vel, dif, xh_send, xh_recv, yh_send, yh_recv,
    xm, ym, xr_send, xr_recv, yr_send, yr_recv, scr, scr_d,
    ins, hs, hr, xms, xmr, xs, xr, yms, ymr, ys, yr,
):
    ncomp, planes, nx, ny = vel.shape
    tx, ty = nx // SUB, ny // SUB
    nf = ncomp * planes
    ix, iy = lax.axis_index("gx"), lax.axis_index("gy")
    x_peers = [lax.rem(ix + o, dx) for o in range(1, dx)]
    y_peers = [lax.rem(iy + o, dy) for o in range(1, dy)]

    vel_copy = pltpu.make_async_copy(vel_in, vel, ins.at[0])
    dif_copy = pltpu.make_async_copy(dif_in, dif, ins.at[1])
    vel_copy.start()
    dif_copy.start()
    barrier = pltpu.get_barrier_semaphore()
    for peer in x_peers:
        pl.semaphore_signal(barrier, inc=1, device_id={"gx": peer}, device_id_type=MESH)
    for peer in y_peers:
        pl.semaphore_signal(barrier, inc=1, device_id={"gy": peer}, device_id_type=MESH)

    def copy(src, dst, send, recv, where):
        return pltpu.make_async_remote_copy(
            src_ref=src, dst_ref=dst, send_sem=send, recv_sem=recv,
            device_id=where, device_id_type=MESH,
        )

    def wide(a):
        return a[:, None]

    row = lax.broadcasted_iota(jnp.int32, (SUB, ny), 0)
    row_y = lax.broadcasted_iota(jnp.int32, (SUB, nx), 0)
    lane = lax.broadcasted_iota(jnp.int32, (nx, ny), 1)
    scale = 0.5 * courant

    vel_copy.wait()
    v = jnp.stack([vel[:, :, pl.ds(t, SUB, stride=tx), :] for t in range(tx)])
    fields = [v[:, c, p].reshape(nx, ny) for c in range(ncomp) for p in range(planes)]
    for f in range(nf):
        ref = vel.at[f // planes, f % planes]
        xh_send[0, f : f + 1, :] = ref[nx - 1 : nx, :]
        xh_send[1, f : f + 1, :] = ref[0:1, :]
    edges = jnp.zeros((nx, ny), jnp.float32)
    for f, a in enumerate(fields):
        edges = jnp.where(lane // 2 == f, pltpu.roll(a, 2 * f + 1, 1), edges)
    yh_send[...] = edges.T[: 2 * SUB]

    x_high, x_low = {"gx": lax.rem(ix + 1, dx)}, {"gx": lax.rem(ix + dx - 1, dx)}
    y_high, y_low = {"gy": lax.rem(iy + 1, dy)}, {"gy": lax.rem(iy + dy - 1, dy)}
    halos = [
        (copy(yh_send, yh_recv.at[0], hs.at[2], hr.at[2], y_high), iy < dy - 1, iy > 0),
        (copy(yh_send, yh_recv.at[1], hs.at[3], hr.at[3], y_low), iy > 0, iy < dy - 1),
        (copy(xh_send.at[0], xh_recv.at[0], hs.at[0], hr.at[0], x_high), ix < dx - 1, ix > 0),
        (copy(xh_send.at[1], xh_recv.at[1], hs.at[1], hr.at[1], x_low), ix > 0, ix < dx - 1),
    ]
    pl.semaphore_wait(barrier, dx + dy - 2)
    for c, sends, takes in halos:
        pl.when(sends)(c.start)

    dif_copy.wait()
    d = jnp.stack([dif[:, pl.ds(t, SUB, stride=tx), :] for t in range(tx)])
    xt, c, gl, gr = tree_matrix(d, row)
    xrow, c, gl, gr = rows_matrix(c, gl, gr)
    put_matrix(
        xm, ix, c, gl, gr, [dif[p, 0:1, :] for p in range(planes)],
        [dif[p, nx - 1 : nx, :] for p in range(planes)],
    )
    xm_copies = [
        copy(xm.at[ix], xm.at[ix], xms.at[o], xmr.at[o], {"gx": peer})
        for o, peer in enumerate(x_peers)
    ]
    for c in xm_copies:
        c.start()
    for p in range(planes):
        scr_d[p] = d[:, p].reshape(nx, ny).T
    dt = jnp.stack([scr_d[:, pl.ds(t, SUB, stride=ty), :] for t in range(ty)])
    yt, c, gl, gr = tree_matrix(dt, row_y)
    yrow, c, gl, gr = rows_matrix(c, gl, gr)
    put_matrix(
        ym, iy, c, gl, gr, [scr_d[p, 0:1, :] for p in range(planes)],
        [scr_d[p, ny - 1 : ny, :] for p in range(planes)],
    )
    ym_copies = [
        copy(ym.at[iy], ym.at[iy], yms.at[o], ymr.at[o], {"gy": peer})
        for o, peer in enumerate(y_peers)
    ]
    for c in ym_copies:
        c.start()

    source = []
    for cc in range(ncomp):
        for p in range(planes):
            f = cc * planes + p
            a = v[:, cc, p]
            lo = jnp.where(row == 0, 0.0, pltpu.roll(a[tx - 1], 1, 0))
            hi = jnp.where(row == SUB - 1, 0.0, pltpu.roll(a[0], SUB - 1, 0))
            grad_x = jnp.concatenate([a[1:], hi[None]], 0) - jnp.concatenate([lo[None], a[:-1]], 0)
            grad_y = jnp.where(lane == ny - 1, 0.0, pltpu.roll(fields[f], ny - 1, 1))
            grad_y = grad_y - jnp.where(lane == 0, 0.0, pltpu.roll(fields[f], 1, 1))
            grad_y = grad_y.reshape(tx, SUB, ny)
            source.append(a - scale * (v[:, 0, p] * grad_x + v[:, 1, p] * grad_y))
    side = jnp.where(lane == 0, scale, jnp.where(lane == ny - 1, -scale, 0.0))
    weight = [side * fields[planes + p] for p in range(planes)]

    for c in xm_copies:
        c.wait_recv()
    x_first, x_last, x_inner = ends_matrix(xm, dx, ix, planes, row)

    for c, sends, takes in halos:
        pl.when(takes)(c.wait_recv)
    take = lax.broadcasted_iota(jnp.int32, (2 * SUB, nx), 0) % 2 == 0
    halo = jnp.where(
        take,
        jnp.where(iy < dy - 1, pltpu.roll(yh_recv[1], 2 * SUB - 1, 0), 0.0),
        jnp.where(iy > 0, pltpu.roll(yh_recv[0], 1, 0), 0.0),
    )
    halo = jnp.where(lax.broadcasted_iota(jnp.int32, (2 * SUB, nx), 0) < 2 * nf, halo, 0.0)
    halo = jnp.concatenate([halo, jnp.zeros((ny - 2 * SUB, nx), jnp.float32)], 0).T
    for f in range(nf):
        near = pltpu.roll(halo, ny - 2 * f - 1, 1)
        source[f] = source[f] + (weight[f % planes] * near).reshape(tx, SUB, ny)
    source = jnp.stack(source, 1).reshape(v.shape)
    xmids, il, ir = tree_source(None, source, xt, wide)
    xrowmids, il, ir = rows_source(il, ir, xrow)
    own_first = pick(row % planes, [xh_send[1, p : p + 1, :] for p in range(planes)])
    own_last = pick(row % planes, [xh_send[0, p : p + 1, :] for p in range(planes)])
    il = tile_of(il, row) + scale * own_first * jnp.where(ix > 0, xh_recv[0], 0.0)
    ir = tile_of(ir, row) - scale * own_last * jnp.where(ix < dx - 1, xh_recv[1], 0.0)
    x_copies = [
        copy(xr_send.at[peer], xr_recv.at[ix], xs.at[o], xr.at[o], {"gx": peer})
        for o, peer in enumerate(x_peers)
    ]
    ends_send(xr_send, il, ir, x_first, x_last, x_copies)

    for c in ym_copies:
        c.wait_recv()
    y_first, y_last, y_inner = ends_matrix(ym, dy, iy, planes, row_y)

    for c in x_copies:
        c.wait_recv()
    low, high = ends_solve(xr_recv, il, ir, x_inner, dx, ix, ncomp, planes)
    left, right = rows_down(low, high, xrow, xrowmids, row)
    middle = tree_down(left, right, xt, xmids, wide)

    for f in range(nf):
        cc, p = f // planes, f % planes
        scr[cc, p] = middle[:, cc, p].reshape(nx, ny).T
    m = jnp.stack([scr[:, :, pl.ds(t, SUB, stride=ty), :] for t in range(ty)])
    ymids, il, ir = tree_source(None, m, yt, wide)
    yrowmids, il, ir = rows_source(il, ir, yrow)
    il, ir = tile_of(il, row_y), tile_of(ir, row_y)
    y_copies = [
        copy(yr_send.at[peer], yr_recv.at[iy], ys.at[o], yr.at[o], {"gy": peer})
        for o, peer in enumerate(y_peers)
    ]
    ends_send(yr_send, il, ir, y_first, y_last, y_copies)
    for c in y_copies:
        c.wait_recv()
    low, high = ends_solve(yr_recv, il, ir, y_inner, dy, iy, ncomp, planes)
    left, right = rows_down(low, high, yrow, yrowmids, row_y)
    w = tree_down(left, right, yt, ymids, wide)
    for t in range(ty):
        scr[:, :, pl.ds(t, SUB, stride=ty), :] = w[t]
    for f in range(nf):
        cc, p = f // planes, f % planes
        a = scr[cc, p].T.reshape(tx, SUB, ny)
        for t in range(tx):
            out[cc, p, pl.ds(t, SUB, stride=tx), :] = a[t]

    for c, sends, takes in halos:
        pl.when(sends)(c.wait_send)
    for c in xm_copies + ym_copies + x_copies + y_copies:
        c.wait_send()


def local(dx, dy, velocity, diffusion):
    ncomp, planes, nx, ny = velocity.shape
    vmem = pl.BlockSpec(memory_space=pltpu.VMEM)
    f32 = jnp.float32
    dma = pltpu.SemaphoreType.DMA
    return pl.pallas_call(
        functools.partial(kernel, dx, dy),
        out_shape=jax.ShapeDtypeStruct(velocity.shape, f32),
        in_specs=[pl.BlockSpec(memory_space=pl.ANY)] * 2,
        out_specs=vmem,
        scratch_shapes=[
            pltpu.VMEM(velocity.shape, f32),
            pltpu.VMEM(diffusion.shape, f32),
            pltpu.VMEM((2, SUB, ny), f32),
            pltpu.VMEM((2, SUB, ny), f32),
            pltpu.VMEM((2 * SUB, nx), f32),
            pltpu.VMEM((2, 2 * SUB, nx), f32),
            pltpu.VMEM((dx, 2 * SUB, ny), f32),
            pltpu.VMEM((dy, 2 * SUB, nx), f32),
            pltpu.VMEM((dx, SUB, ny), f32),
            pltpu.VMEM((dx, SUB, ny), f32),
            pltpu.VMEM((dy, SUB, nx), f32),
            pltpu.VMEM((dy, SUB, nx), f32),
            pltpu.VMEM((ncomp, planes, ny, nx), f32),
            pltpu.VMEM((planes, ny, nx), f32),
            dma((2,)), dma((4,)), dma((4,)),
            dma((dx,)), dma((dx,)), dma((dx,)), dma((dx,)),
            dma((dy,)), dma((dy,)), dma((dy,)), dma((dy,)),
        ],
        compiler_params=pltpu.CompilerParams(
            collective_id=0, has_side_effects=True, vmem_limit_bytes=60 * 1024 * 1024
        ),
    )(velocity, diffusion)


def solution(mesh):
    in_specs = (P(None, None, "gx", "gy"), P(None, "gx", "gy"))
    out_specs = P(None, None, "gx", "gy")
    body = functools.partial(local, mesh.shape["gx"], mesh.shape["gy"])
    return jax.shard_map(body, mesh=mesh, in_specs=in_specs, out_specs=out_specs, check_vma=False)
```

time: 19.2 us -> 19.7 us (1.026)
  Pallas kernels: 16.4 us -> 17.7 us
  local copies, waits for them, and re-layouts: 2.65 us -> 1.77 us
    pallas_call x1, Pallas kernels: 16.4 us -> 17.7 us  [local(): pl.pallas_call(functools.partial(kernel, dx, dy), out_shape=jax.ShapeDtyp...]
    unnamed x5 -> x1, local copies, waits for them, and re-layouts: 2.65 us -> 1.77 us
where the time goes in v2:
time: 19.7 us; the launch traced here: 19.5 us
  Pallas kernels  17.7 us (90%)
  local copies, waits for them, and re-layouts  1.77 us (9%)
    pallas_call x1, Pallas kernels, local(): pl.pallas_call(functools.partial(kernel, dx, dy), out_shape=jax.ShapeDtyp...  17.7 us
    unnamed x1, local copies, waits for them, and re-layouts  1.77 us

profile of v2, /device:TPU:0, one launch (start us, length us, event | category | flops | bytes accessed | tf_op | source)
XLA Modules:
  0.0 19.5 jit_solution(6636405063105816067)
XLA Ops:
  0.0 17.7 %shard_map.28 = f32[3,2,128,128]{3,2,1,0:T(8,128)} custom-call(f32[3,2,128,128]{3,2,1,0:T(8,128)} %vel_in.1, f32[2,128,128]{2,1,0:T(8,128)} %dif_in.1), custom_call_target="tpu_custom_call" | custom-call | tf_op jit(solution)/shard_map/pallas_call | solution.py:391
  17.7 1.8 %copy.4 = f32[3,2,128,128]{3,2,1,0:T(8,128)} copy(f32[3,2,128,128]{3,2,1,0:T(8,128)} %shard_map.28) | data formatting | bytes 786432

commit v3 on v2

--- a/solution.py
+++ b/solution.py
@@ -207,8 +207,8 @@
 
 
 def kernel(
-    dx, dy, vel_in, dif_in, out,
-    vel, dif, xh_send, xh_recv, yh_send, yh_recv,
+    dx, dy, vel_in, dif, out,
+    vel, xh_send, xh_recv, yh_send, yh_recv,
     xm, ym, xr_send, xr_recv, yr_send, yr_recv, scr, scr_d,
     ins, hs, hr, xms, xmr, xs, xr, yms, ymr, ys, yr,
 ):
@@ -220,9 +220,7 @@
     y_peers = [lax.rem(iy + o, dy) for o in range(1, dy)]
 
     vel_copy = pltpu.make_async_copy(vel_in, vel, ins.at[0])
-    dif_copy = pltpu.make_async_copy(dif_in, dif, ins.at[1])
     vel_copy.start()
-    dif_copy.start()
     barrier = pltpu.get_barrier_semaphore()
     for peer in x_peers:
         pl.semaphore_signal(barrier, inc=1, device_id={"gx": peer}, device_id_type=MESH)
@@ -242,6 +240,23 @@
     row_y = lax.broadcasted_iota(jnp.int32, (SUB, nx), 0)
     lane = lax.broadcasted_iota(jnp.int32, (nx, ny), 1)
     scale = 0.5 * courant
+
+    d = jnp.stack([dif[:, pl.ds(t, SUB, stride=tx), :] for t in range(tx)])
+    xt, c, gl, gr = tree_matrix(d, row)
+    xrow, c, gl, gr = rows_matrix(c, gl, gr)
+    put_matrix(
+        xm, ix, c, gl, gr, [dif[p, 0:1, :] for p in range(planes)],
+        [dif[p, nx - 1 : nx, :] for p in range(planes)],
+    )
+    for p in range(planes):
+        scr_d[p] = d[:, p].reshape(nx, ny).T
+    dt = jnp.stack([scr_d[:, pl.ds(t, SUB, stride=ty), :] for t in range(ty)])
+    yt, c, gl, gr = tree_matrix(dt, row_y)
+    yrow, c, gl, gr = rows_matrix(c, gl, gr)
+    put_matrix(
+        ym, iy, c, gl, gr, [scr_d[p, 0:1, :] for p in range(planes)],
+        [scr_d[p, ny - 1 : ny, :] for p in range(planes)],
+    )
 
     vel_copy.wait()
     v = jnp.stack([vel[:, :, pl.ds(t, SUB, stride=tx), :] for t in range(tx)])
@@ -267,29 +282,12 @@
     for c, sends, takes in halos:
         pl.when(sends)(c.start)
 
-    dif_copy.wait()
-    d = jnp.stack([dif[:, pl.ds(t, SUB, stride=tx), :] for t in range(tx)])
-    xt, c, gl, gr = tree_matrix(d, row)
-    xrow, c, gl, gr = rows_matrix(c, gl, gr)
-    put_matrix(
-        xm, ix, c, gl, gr, [dif[p, 0:1, :] for p in range(planes)],
-        [dif[p, nx - 1 : nx, :] for p in range(planes)],
-    )
     xm_copies = [
         copy(xm.at[ix], xm.at[ix], xms.at[o], xmr.at[o], {"gx": peer})
         for o, peer in enumerate(x_peers)
     ]
     for c in xm_copies:
         c.start()
-    for p in range(planes):
-        scr_d[p] = d[:, p].reshape(nx, ny).T
-    dt = jnp.stack([scr_d[:, pl.ds(t, SUB, stride=ty), :] for t in range(ty)])
-    yt, c, gl, gr = tree_matrix(dt, row_y)
-    yrow, c, gl, gr = rows_matrix(c, gl, gr)
-    put_matrix(
-        ym, iy, c, gl, gr, [scr_d[p, 0:1, :] for p in range(planes)],
-        [scr_d[p, ny - 1 : ny, :] for p in range(planes)],
-    )
     ym_copies = [
         copy(ym.at[iy], ym.at[iy], yms.at[o], ymr.at[o], {"gy": peer})
         for o, peer in enumerate(y_peers)
@@ -391,11 +389,10 @@
     return pl.pallas_call(
         functools.partial(kernel, dx, dy),
         out_shape=jax.ShapeDtypeStruct(velocity.shape, f32),
-        in_specs=[pl.BlockSpec(memory_space=pl.ANY)] * 2,
+        in_specs=[pl.BlockSpec(memory_space=pl.ANY), vmem],
         out_specs=vmem,
         scratch_shapes=[
             pltpu.VMEM(velocity.shape, f32),
-            pltpu.VMEM(diffusion.shape, f32),
             pltpu.VMEM((2, SUB, ny), f32),
             pltpu.VMEM((2, SUB, ny), f32),
             pltpu.VMEM((2 * SUB, nx), f32),
@@ -408,12 +405,12 @@
             pltpu.VMEM((dy, SUB, nx), f32),
             pltpu.VMEM((ncomp, planes, ny, nx), f32),
             pltpu.VMEM((planes, ny, nx), f32),
-            dma((2,)), dma((4,)), dma((4,)),
+            dma((1,)), dma((4,)), dma((4,)),
             dma((dx,)), dma((dx,)), dma((dx,)), dma((dx,)),
             dma((dy,)), dma((dy,)), dma((dy,)), dma((dy,)),
         ],
         compiler_params=pltpu.CompilerParams(
-            collective_id=0, has_side_effects=True, vmem_limit_bytes=60 * 1024 * 1024
+            collective_id=0, has_side_effects=True, vmem_limit_bytes=54592 * 1024
         ),
     )(velocity, diffusion)
 

time: 19.7 us -> 18.8 us (0.954)
  Pallas kernels: 17.7 us -> 17 us
    pallas_call x1, Pallas kernels: 17.7 us -> 17 us  [local(): pl.pallas_call(functools.partial(kernel, dx, dy), out_shape=jax.ShapeDtyp...]
    unnamed x1 -> x3, local copies, waits for them, and re-layouts: 1.77 us -> 1.65 us
where the time goes in v3:
time: 18.8 us; the launch traced here: 18.7 us
  Pallas kernels  17 us (90%)
  local copies, waits for them, and re-layouts  1.65 us (9%)
    pallas_call x1, Pallas kernels, local(): pl.pallas_call(functools.partial(kernel, dx, dy), out_shape=jax.ShapeDtyp...  17 us
    unnamed x3, local copies, waits for them, and re-layouts  1.65 us

profile of v3, /device:TPU:0, one launch (start us, length us, event | category | flops | bytes accessed | tf_op | source)
XLA Modules:
  0.0 18.7 jit_solution(5683265868992417793)
XLA Ops:
  0.0 0.0 copy-start
  0.0 0.9 %copy-done = f32[2,128,128]{2,1,0:T(8,128)S(1)} copy-done((f32[2,128,128]{2,1,0:T(8,128)S(1)}, f32[2,128,128]{2,1,0:T(8,128)}, u32[]{:S(2)}) %copy-start) | copy-done | bytes 131096
  0.9 17.0 %shard_map.28 = f32[3,2,128,128]{3,2,1,0:T(8,128)S(1)} custom-call(f32[3,2,128,128]{3,2,1,0:T(8,128)} %vel_in.1, f32[2,128,128]{2,1,0:T(8,128)S(1)} %copy-done), custom_call_target="tpu_custom_call" | custom-call | tf_op jit(solution)/shard_map/pallas_call | solution.py:389
  17.9 0.7 %copy.4 = f32[3,2,128,128]{3,2,1,0:T(8,128)} copy(f32[3,2,128,128]{3,2,1,0:T(8,128)S(1)} %shard_map.28) | data formatting | bytes 786432
Async XLA Ops:
  0.0 0.9 %copy-start = (f32[2,128,128]{2,1,0:T(8,128)S(1)}, f32[2,128,128]{2,1,0:T(8,128)}, u32[]{:S(2)}) copy-start(f32[2,128,128]{2,1,0:T(8,128)} %dif.1) | copy-start | bytes 393220

commit v4 on v3

--- a/solution.py
+++ b/solution.py
@@ -248,15 +248,6 @@
         xm, ix, c, gl, gr, [dif[p, 0:1, :] for p in range(planes)],
         [dif[p, nx - 1 : nx, :] for p in range(planes)],
     )
-    for p in range(planes):
-        scr_d[p] = d[:, p].reshape(nx, ny).T
-    dt = jnp.stack([scr_d[:, pl.ds(t, SUB, stride=ty), :] for t in range(ty)])
-    yt, c, gl, gr = tree_matrix(dt, row_y)
-    yrow, c, gl, gr = rows_matrix(c, gl, gr)
-    put_matrix(
-        ym, iy, c, gl, gr, [scr_d[p, 0:1, :] for p in range(planes)],
-        [scr_d[p, ny - 1 : ny, :] for p in range(planes)],
-    )
 
     vel_copy.wait()
     v = jnp.stack([vel[:, :, pl.ds(t, SUB, stride=tx), :] for t in range(tx)])
@@ -288,6 +279,15 @@
     ]
     for c in xm_copies:
         c.start()
+    for p in range(planes):
+        scr_d[p] = d[:, p].reshape(nx, ny).T
+    dt = jnp.stack([scr_d[:, pl.ds(t, SUB, stride=ty), :] for t in range(ty)])
+    yt, c, gl, gr = tree_matrix(dt, row_y)
+    yrow, c, gl, gr = rows_matrix(c, gl, gr)
+    put_matrix(
+        ym, iy, c, gl, gr, [scr_d[p, 0:1, :] for p in range(planes)],
+        [scr_d[p, ny - 1 : ny, :] for p in range(planes)],
+    )
     ym_copies = [
         copy(ym.at[iy], ym.at[iy], yms.at[o], ymr.at[o], {"gy": peer})
         for o, peer in enumerate(y_peers)
@@ -362,6 +362,10 @@
         for o, peer in enumerate(y_peers)
     ]
     ends_send(yr_send, il, ir, y_first, y_last, y_copies)
+    for c, sends, takes in halos:
+        pl.when(sends)(c.wait_send)
+    for c in xm_copies + ym_copies + x_copies + y_copies:
+        c.wait_send()
     for c in y_copies:
         c.wait_recv()
     low, high = ends_solve(yr_recv, il, ir, y_inner, dy, iy, ncomp, planes)
@@ -374,11 +378,6 @@
         a = scr[cc, p].T.reshape(tx, SUB, ny)
         for t in range(tx):
             out[cc, p, pl.ds(t, SUB, stride=tx), :] = a[t]
-
-    for c, sends, takes in halos:
-        pl.when(sends)(c.wait_send)
-    for c in xm_copies + ym_copies + x_copies + y_copies:
-        c.wait_send()
 
 
 def local(dx, dy, velocity, diffusion):

time: 18.8 us -> 18.7 us (level)
  no operation moved by 1% of the time
where the time goes in v4:
time: 18.7 us; the launch traced here: 18.5 us
  Pallas kernels  16.9 us (90%)
  local copies, waits for them, and re-layouts  1.65 us (9%)
    pallas_call x1, Pallas kernels, local(): pl.pallas_call(functools.partial(kernel, dx, dy), out_shape=jax.ShapeDtyp...  16.9 us
    unnamed x3, local copies, waits for them, and re-layouts  1.65 us

profile of v4, /device:TPU:0, one launch (start us, length us, event | category | flops | bytes accessed | tf_op | source)
XLA Modules:
  0.0 18.5 jit_solution(17899125356759930328)
XLA Ops:
  0.0 0.0 copy-start
  0.0 0.9 %copy-done = f32[2,128,128]{2,1,0:T(8,128)S(1)} copy-done((f32[2,128,128]{2,1,0:T(8,128)S(1)}, f32[2,128,128]{2,1,0:T(8,128)}, u32[]{:S(2)}) %copy-start) | copy-done | bytes 131096
  0.9 16.9 %shard_map.28 = f32[3,2,128,128]{3,2,1,0:T(8,128)S(1)} custom-call(f32[3,2,128,128]{3,2,1,0:T(8,128)} %vel_in.1, f32[2,128,128]{2,1,0:T(8,128)S(1)} %copy-done), custom_call_target="tpu_custom_call" | custom-call | tf_op jit(solution)/shard_map/pallas_call | solution.py:388
  17.8 0.7 %copy.4 = f32[3,2,128,128]{3,2,1,0:T(8,128)} copy(f32[3,2,128,128]{3,2,1,0:T(8,128)S(1)} %shard_map.28) | data formatting | bytes 786432
Async XLA Ops:
  0.0 0.9 %copy-start = (f32[2,128,128]{2,1,0:T(8,128)S(1)}, f32[2,128,128]{2,1,0:T(8,128)}, u32[]{:S(2)}) copy-start(f32[2,128,128]{2,1,0:T(8,128)} %dif.1) | copy-start | bytes 393220

commit v5 on v2

--- a/solution.py
+++ b/solution.py
@@ -364,6 +364,10 @@
         for o, peer in enumerate(y_peers)
     ]
     ends_send(yr_send, il, ir, y_first, y_last, y_copies)
+    for c, sends, takes in halos:
+        pl.when(sends)(c.wait_send)
+    for c in xm_copies + ym_copies + x_copies + y_copies:
+        c.wait_send()
     for c in y_copies:
         c.wait_recv()
     low, high = ends_solve(yr_recv, il, ir, y_inner, dy, iy, ncomp, planes)
@@ -377,11 +381,6 @@
         for t in range(tx):
             out[cc, p, pl.ds(t, SUB, stride=tx), :] = a[t]
 
-    for c, sends, takes in halos:
-        pl.when(sends)(c.wait_send)
-    for c in xm_copies + ym_copies + x_copies + y_copies:
-        c.wait_send()
-
 
 def local(dx, dy, velocity, diffusion):
     ncomp, planes, nx, ny = velocity.shape
@@ -390,8 +389,8 @@
     dma = pltpu.SemaphoreType.DMA
     return pl.pallas_call(
         functools.partial(kernel, dx, dy),
-        out_shape=jax.ShapeDtypeStruct(velocity.shape, f32),
-        in_specs=[pl.BlockSpec(memory_space=pl.ANY)] * 2,
+        out_shape=pltpu.VMEM(velocity.shape, f32),
+        in_specs=[pl.BlockSpec(memory_space=pltpu.HBM)] * 2,
         out_specs=vmem,
         scratch_shapes=[
             pltpu.VMEM(velocity.shape, f32),
@@ -413,9 +412,12 @@
             dma((dy,)), dma((dy,)), dma((dy,)), dma((dy,)),
         ],
         compiler_params=pltpu.CompilerParams(
-            collective_id=0, has_side_effects=True, vmem_limit_bytes=60 * 1024 * 1024
+            collective_id=0, has_side_effects=True, vmem_limit_bytes=32 * 1024 * 1024
         ),
-    )(velocity, diffusion)
+    )(
+        pltpu.with_memory_space_constraint(velocity, pltpu.HBM),
+        pltpu.with_memory_space_constraint(diffusion, pltpu.HBM),
+    )
 
 
 def solution(mesh):

time: 19.7 us -> 17.9 us (0.909)
  local copies, waits for them, and re-layouts: 1.77 us -> 0.75 us
  Pallas kernels: 17.7 us -> 17 us
    unnamed x1, local copies, waits for them, and re-layouts: 1.77 us -> 0.75 us
    pallas_call x1, Pallas kernels: 17.7 us -> 17 us  [local(): pl.pallas_call(functools.partial(kernel, dx, dy), out_shape=pltpu.VMEM(ve...]
where the time goes in v5:
time: 17.9 us; the launch traced here: 17.7 us
  Pallas kernels  17 us (95%)
  local copies, waits for them, and re-layouts  0.75 us (4%)
    pallas_call x1, Pallas kernels, local(): pl.pallas_call(functools.partial(kernel, dx, dy), out_shape=pltpu.VMEM(ve...  17 us
    unnamed x1, local copies, waits for them, and re-layouts  0.75 us

profile of v5, /device:TPU:0, one launch (start us, length us, event | category | flops | bytes accessed | tf_op | source)
XLA Modules:
  0.0 17.7 jit_solution(16944780531622459674)
XLA Ops:
  0.0 17.0 %shard_map.28 = f32[3,2,128,128]{3,2,1,0:T(8,128)S(1)} custom-call(f32[3,2,128,128]{3,2,1,0:T(8,128)} %vel_in.1, f32[2,128,128]{2,1,0:T(8,128)} %dif_in.1), custom_call_target="tpu_custom_call" | custom-call | tf_op jit(solution)/shard_map/pallas_call | solution.py:390
  17.0 0.7 %copy.4 = f32[3,2,128,128]{3,2,1,0:T(8,128)} copy(f32[3,2,128,128]{3,2,1,0:T(8,128)S(1)} %shard_map.28) | data formatting | bytes 786432

commit v6 on v5

--- a/solution.py
+++ b/solution.py
@@ -116,6 +116,23 @@
     return jnp.where(row == 0, left, roll_rows(w, 1)), w
 
 
+def end_shapes(levels, row_levels, row):
+    one = jnp.ones_like(row_levels[0][0])
+    out = []
+    for left, right in ((one, 0.0 * one), (0.0 * one, one)):
+        low, high = rows_down(left, right, row_levels, [0.0] * 3, row)
+        out.append(tree_down(low, high, levels, [0.0] * len(levels), lambda a: a))
+    return out
+
+
+def inner_part(source, levels, row_levels, row, widen):
+    mids, il, ir = tree_source(None, source, levels, widen)
+    row_mids, il, ir = rows_source(il, ir, row_levels)
+    zero = jnp.zeros_like(il)
+    low, high = rows_down(zero, zero, row_levels, row_mids, row)
+    return tree_down(low, high, levels, mids, widen)
+
+
 def pick(place, items):
     out = items[0]
     for k in range(1, len(items)):
@@ -127,7 +144,7 @@
     flat = a.reshape((-1,) + a.shape[-2:])
     out = jnp.zeros_like(flat[0])
     for f in range(flat.shape[0]):
-        out = jnp.where(row == f, pltpu.roll(flat[f], (f + 1) % SUB, 0), out)
+        out = jnp.where(row == f, jnp.sum(flat[f], axis=0, keepdims=True), out)
     return out
 
 
@@ -191,7 +208,7 @@
         c.start()
 
 
-def ends_solve(recv, il, ir, inner, count, place, ncomp, planes):
+def ends_solve(recv, il, ir, inner, count, place):
     for k in range(count):
         tile = recv[k]
         il = il + jnp.where(k < place, tile, 0.0)
@@ -199,11 +216,7 @@
     low = inner[0] * il + inner[1] * ir
     high = inner[1] * il + inner[2] * ir
 
-    def split(a):
-        parts = [jnp.broadcast_to(a[f : f + 1], a.shape) for f in range(ncomp * planes)]
-        return jnp.stack(parts).reshape((ncomp, planes) + a.shape)
-
-    return split(low), split(high)
+    return low, high
 
 
 def kernel(
@@ -312,6 +325,7 @@
     side = jnp.where(lane == 0, scale, jnp.where(lane == ny - 1, -scale, 0.0))
     weight = [side * fields[planes + p] for p in range(planes)]
 
+    x_left, x_right = end_shapes(xt, xrow, row)
     for c in xm_copies:
         c.wait_recv()
     x_first, x_last, x_inner = ends_matrix(xm, dx, ix, planes, row)
@@ -330,12 +344,10 @@
         near = pltpu.roll(halo, ny - 2 * f - 1, 1)
         source[f] = source[f] + (weight[f % planes] * near).reshape(tx, SUB, ny)
     source = jnp.stack(source, 1).reshape(v.shape)
-    xmids, il, ir = tree_source(None, source, xt, wide)
-    xrowmids, il, ir = rows_source(il, ir, xrow)
     own_first = pick(row % planes, [xh_send[1, p : p + 1, :] for p in range(planes)])
     own_last = pick(row % planes, [xh_send[0, p : p + 1, :] for p in range(planes)])
-    il = tile_of(il, row) + scale * own_first * jnp.where(ix > 0, xh_recv[0], 0.0)
-    ir = tile_of(ir, row) - scale * own_last * jnp.where(ix < dx - 1, xh_recv[1], 0.0)
+    il = tile_of(jnp.sum(wide(x_left) * source, axis=0), row) + scale * own_first * jnp.where(ix > 0, xh_recv[0], 0.0)
+    ir = tile_of(jnp.sum(wide(x_right) * source, axis=0), row) - scale * own_last * jnp.where(ix < dx - 1, xh_recv[1], 0.0)
     x_copies = [
         copy(xr_send.at[peer], xr_recv.at[ix], xs.at[o], xr.at[o], {"gx": peer})
         for o, peer in enumerate(x_peers)
@@ -346,40 +358,60 @@
         c.wait_recv()
     y_first, y_last, y_inner = ends_matrix(ym, dy, iy, planes, row_y)
 
+    middle = inner_part(source, xt, xrow, row, wide)
+    shapes = []
+    for shape in end_shapes(yt, yrow, row_y):
+        for t in range(ty):
+            scr_d[:, pl.ds(t, SUB, stride=ty), :] = shape[t]
+        shapes.append([scr_d[p].T for p in range(planes)])
+    y_left, y_right = shapes
+
     for c in x_copies:
         c.wait_recv()
-    low, high = ends_solve(xr_recv, il, ir, x_inner, dx, ix, ncomp, planes)
-    left, right = rows_down(low, high, xrow, xrowmids, row)
-    middle = tree_down(left, right, xt, xmids, wide)
-
-    for f in range(nf):
-        cc, p = f // planes, f % planes
-        scr[cc, p] = middle[:, cc, p].reshape(nx, ny).T
-    m = jnp.stack([scr[:, :, pl.ds(t, SUB, stride=ty), :] for t in range(ty)])
-    ymids, il, ir = tree_source(None, m, yt, wide)
-    yrowmids, il, ir = rows_source(il, ir, yrow)
-    il, ir = tile_of(il, row_y), tile_of(ir, row_y)
+    low, high = ends_solve(xr_recv, il, ir, x_inner, dx, ix)
+    middle = [
+        middle[:, f // planes, f % planes]
+        + x_left[:, f % planes] * low[f : f + 1]
+        + x_right[:, f % planes] * high[f : f + 1]
+        for f in range(nf)
+    ]
+    middle = [a.reshape(nx, ny) for a in middle]
+    ends = jnp.zeros((nx, ny), jnp.float32)
+    for f, a in enumerate(middle):
+        at_left = jnp.sum(a * y_left[f % planes], axis=1, keepdims=True)
+        at_right = jnp.sum(a * y_right[f % planes], axis=1, keepdims=True)
+        ends = jnp.where(lane == f, at_left, jnp.where(lane == SUB + f, at_right, ends))
+    ends = ends.T
+    il, ir = ends[:SUB], ends[SUB : 2 * SUB]
     y_copies = [
         copy(yr_send.at[peer], yr_recv.at[iy], ys.at[o], yr.at[o], {"gy": peer})
         for o, peer in enumerate(y_peers)
     ]
     ends_send(yr_send, il, ir, y_first, y_last, y_copies)
+
+    for f in range(nf):
+        scr[f // planes, f % planes] = middle[f].T
+    m = jnp.stack([scr[:, :, pl.ds(t, SUB, stride=ty), :] for t in range(ty)])
+    w = inner_part(m, yt, yrow, row_y, wide)
+    for t in range(ty):
+        scr[:, :, pl.ds(t, SUB, stride=ty), :] = w[t]
+    w = [scr[f // planes, f % planes].T for f in range(nf)]
     for c, sends, takes in halos:
         pl.when(sends)(c.wait_send)
     for c in xm_copies + ym_copies + x_copies + y_copies:
         c.wait_send()
+
     for c in y_copies:
         c.wait_recv()
-    low, high = ends_solve(yr_recv, il, ir, y_inner, dy, iy, ncomp, planes)
-    left, right = rows_down(low, high, yrow, yrowmids, row_y)
-    w = tree_down(left, right, yt, ymids, wide)
-    for t in range(ty):
-        scr[:, :, pl.ds(t, SUB, stride=ty), :] = w[t]
+    low, high = ends_solve(yr_recv, il, ir, y_inner, dy, iy)
+    blank = jnp.zeros((ny - 2 * SUB, nx), jnp.float32)
+    ends = jnp.concatenate([low, high, blank], 0).T
     for f in range(nf):
-        cc, p = f // planes, f % planes
-        a = scr[cc, p].T.reshape(tx, SUB, ny)
+        p = f % planes
+        a = w[f] + y_left[p] * ends[:, f : f + 1] + y_right[p] * ends[:, SUB + f : SUB + f + 1]
+        a = a.reshape(tx, SUB, ny)
         for t in range(tx):
-            out[cc, p, pl.ds(t, SUB, stride=tx), :] = a[t]
+            out[f // planes, p, pl.ds(t, SUB, stride=tx), :] = a[t]
 
 
 def local(dx, dy, velocity, diffusion):

time: 17.9 us -> 18 us (level)
  no operation moved by 1% of the time
where the time goes in v6:
time: 18 us; the launch traced here: 17.9 us
  Pallas kernels  17.1 us (95%)
  local copies, waits for them, and re-layouts  0.75 us (4%)
    pallas_call x1, Pallas kernels, local(): pl.pallas_call(functools.partial(kernel, dx, dy), out_shape=pltpu.VMEM(ve...  17.1 us
    unnamed x1, local copies, waits for them, and re-layouts  0.75 us

profile of v6, /device:TPU:0, one launch (start us, length us, event | category | flops | bytes accessed | tf_op | source)
XLA Modules:
  0.0 17.9 jit_solution(8964102398349677793)
XLA Ops:
  0.0 17.1 %shard_map.28 = f32[3,2,128,128]{3,2,1,0:T(8,128)S(1)} custom-call(f32[3,2,128,128]{3,2,1,0:T(8,128)} %vel_in.1, f32[2,128,128]{2,1,0:T(8,128)} %dif_in.1), custom_call_target="tpu_custom_call" | custom-call | tf_op jit(solution)/shard_map/pallas_call | solution.py:422
  17.1 0.7 %copy.4 = f32[3,2,128,128]{3,2,1,0:T(8,128)} copy(f32[3,2,128,128]{3,2,1,0:T(8,128)S(1)} %shard_map.28) | data formatting | bytes 786432

commit v7 on v6

--- a/solution.py
+++ b/solution.py
@@ -137,14 +137,6 @@
     out = items[0]
     for k in range(1, len(items)):
         out = jnp.where(place == k, items[k], out)
-    return out
-
-
-def tile_of(a, row):
-    flat = a.reshape((-1,) + a.shape[-2:])
-    out = jnp.zeros_like(flat[0])
-    for f in range(flat.shape[0]):
-        out = jnp.where(row == f, jnp.sum(flat[f], axis=0, keepdims=True), out)
     return out
 
 
@@ -222,7 +214,7 @@
 def kernel(
     dx, dy, vel_in, dif_in, out,
     vel, dif, xh_send, xh_recv, yh_send, yh_recv,
-    xm, ym, xr_send, xr_recv, yr_send, yr_recv, scr, scr_d,
+    xm, ym, xr_send, xr_recv, yr_send, yr_recv, scr, scr_d, v, src, ends_x,
     ins, hs, hr, xms, xmr, xs, xr, yms, ymr, ys, yr,
 ):
     ncomp, planes, nx, ny = vel.shape
@@ -248,8 +240,8 @@
             device_id=where, device_id_type=MESH,
         )
 
-    def wide(a):
-        return a[:, None]
+    def same(a):
+        return a
 
     row = lax.broadcasted_iota(jnp.int32, (SUB, ny), 0)
     row_y = lax.broadcasted_iota(jnp.int32, (SUB, nx), 0)
@@ -257,15 +249,23 @@
     scale = 0.5 * courant
 
     vel_copy.wait()
-    v = jnp.stack([vel[:, :, pl.ds(t, SUB, stride=tx), :] for t in range(tx)])
-    fields = [v[:, c, p].reshape(nx, ny) for c in range(ncomp) for p in range(planes)]
+    for t in range(tx):
+        v[t] = vel[:, :, pl.ds(t, SUB, stride=tx), :]
+
+    def field(c, p):
+        return v[:, c, p].reshape(nx, ny)
+
     for f in range(nf):
         ref = vel.at[f // planes, f % planes]
         xh_send[0, f : f + 1, :] = ref[nx - 1 : nx, :]
         xh_send[1, f : f + 1, :] = ref[0:1, :]
-    edges = jnp.zeros((nx, ny), jnp.float32)
-    for f, a in enumerate(fields):
-        edges = jnp.where(lane // 2 == f, pltpu.roll(a, 2 * f + 1, 1), edges)
+    def add_edges(k, edges):
+        c = ncomp - 1 - k
+        for p in range(planes - 1, -1, -1):
+            edges = jnp.where(lane < 2, pltpu.roll(field(c, p), 1, 1), pltpu.roll(edges, 2, 1))
+        return edges
+
+    edges = lax.fori_loop(0, ncomp, add_edges, jnp.zeros((nx, ny), jnp.float32))
     yh_send[...] = edges.T[: 2 * SUB]
 
     x_high, x_low = {"gx": lax.rem(ix + 1, dx)}, {"gx": lax.rem(ix + dx - 1, dx)}
@@ -310,20 +310,20 @@
     for c in ym_copies:
         c.start()
 
-    source = []
-    for cc in range(ncomp):
+    @pl.loop(0, ncomp)
+    def _(c):
         for p in range(planes):
-            f = cc * planes + p
-            a = v[:, cc, p]
+            a = v[:, c, p]
+            flat = field(c, p)
             lo = jnp.where(row == 0, 0.0, pltpu.roll(a[tx - 1], 1, 0))
             hi = jnp.where(row == SUB - 1, 0.0, pltpu.roll(a[0], SUB - 1, 0))
             grad_x = jnp.concatenate([a[1:], hi[None]], 0) - jnp.concatenate([lo[None], a[:-1]], 0)
-            grad_y = jnp.where(lane == ny - 1, 0.0, pltpu.roll(fields[f], ny - 1, 1))
-            grad_y = grad_y - jnp.where(lane == 0, 0.0, pltpu.roll(fields[f], 1, 1))
+            grad_y = jnp.where(lane == ny - 1, 0.0, pltpu.roll(flat, ny - 1, 1))
+            grad_y = grad_y - jnp.where(lane == 0, 0.0, pltpu.roll(flat, 1, 1))
             grad_y = grad_y.reshape(tx, SUB, ny)
-            source.append(a - scale * (v[:, 0, p] * grad_x + v[:, 1, p] * grad_y))
+            src[c, :, p] = a - scale * (v[:, 0, p] * grad_x + v[:, 1, p] * grad_y)
+
     side = jnp.where(lane == 0, scale, jnp.where(lane == ny - 1, -scale, 0.0))
-    weight = [side * fields[planes + p] for p in range(planes)]
 
     x_left, x_right = end_shapes(xt, xrow, row)
     for c in xm_copies:
@@ -340,14 +340,25 @@
     )
     halo = jnp.where(lax.broadcasted_iota(jnp.int32, (2 * SUB, nx), 0) < 2 * nf, halo, 0.0)
     halo = jnp.concatenate([halo, jnp.zeros((ny - 2 * SUB, nx), jnp.float32)], 0).T
-    for f in range(nf):
-        near = pltpu.roll(halo, ny - 2 * f - 1, 1)
-        source[f] = source[f] + (weight[f % planes] * near).reshape(tx, SUB, ny)
-    source = jnp.stack(source, 1).reshape(v.shape)
+
+    def add_halo(c, state):
+        near, il, ir = state
+        for p in range(planes):
+            f = c * planes + p
+            a = src[c, :, p] + (side * field(1, p) * near).reshape(tx, SUB, ny)
+            src[c, :, p] = a
+            at_left = jnp.sum(jnp.sum(x_left[:, p] * a, axis=0), axis=0, keepdims=True)
+            at_right = jnp.sum(jnp.sum(x_right[:, p] * a, axis=0), axis=0, keepdims=True)
+            il, ir = jnp.where(row == f, at_left, il), jnp.where(row == f, at_right, ir)
+            near = pltpu.roll(near, ny - 2, 1)
+        return near, il, ir
+
+    blank = jnp.zeros((SUB, ny), jnp.float32)
+    _, il, ir = lax.fori_loop(0, ncomp, add_halo, (pltpu.roll(halo, ny - 1, 1), blank, blank))
     own_first = pick(row % planes, [xh_send[1, p : p + 1, :] for p in range(planes)])
     own_last = pick(row % planes, [xh_send[0, p : p + 1, :] for p in range(planes)])
-    il = tile_of(jnp.sum(wide(x_left) * source, axis=0), row) + scale * own_first * jnp.where(ix > 0, xh_recv[0], 0.0)
-    ir = tile_of(jnp.sum(wide(x_right) * source, axis=0), row) - scale * own_last * jnp.where(ix < dx - 1, xh_recv[1], 0.0)
+    il = il + scale * own_first * jnp.where(ix > 0, xh_recv[0], 0.0)
+    ir = ir - scale * own_last * jnp.where(ix < dx - 1, xh_recv[1], 0.0)
     x_copies = [
         copy(xr_send.at[peer], xr_recv.at[ix], xs.at[o], xr.at[o], {"gx": peer})
         for o, peer in enumerate(x_peers)
@@ -358,7 +369,10 @@
         c.wait_recv()
     y_first, y_last, y_inner = ends_matrix(ym, dy, iy, planes, row_y)
 
-    middle = inner_part(source, xt, xrow, row, wide)
+    @pl.loop(0, ncomp)
+    def _(c):
+        src[c] = inner_part(src[c], xt, xrow, row, same)
+
     shapes = []
     for shape in end_shapes(yt, yrow, row_y):
         for t in range(ty):
@@ -369,19 +383,23 @@
     for c in x_copies:
         c.wait_recv()
     low, high = ends_solve(xr_recv, il, ir, x_inner, dx, ix)
-    middle = [
-        middle[:, f // planes, f % planes]
-        + x_left[:, f % planes] * low[f : f + 1]
-        + x_right[:, f % planes] * high[f : f + 1]
-        for f in range(nf)
-    ]
-    middle = [a.reshape(nx, ny) for a in middle]
-    ends = jnp.zeros((nx, ny), jnp.float32)
-    for f, a in enumerate(middle):
-        at_left = jnp.sum(a * y_left[f % planes], axis=1, keepdims=True)
-        at_right = jnp.sum(a * y_right[f % planes], axis=1, keepdims=True)
-        ends = jnp.where(lane == f, at_left, jnp.where(lane == SUB + f, at_right, ends))
-    ends = ends.T
+    ends_x[0], ends_x[1] = low, high
+
+    def add_ends(k, ends):
+        c = ncomp - 1 - k
+        for p in range(planes - 1, -1, -1):
+            f = c * planes + p
+            a = src[c, :, p] + x_left[:, p] * ends_x[0, pl.ds(f, 1), :]
+            a = a + x_right[:, p] * ends_x[1, pl.ds(f, 1), :]
+            src[c, :, p] = a
+            a = a.reshape(nx, ny)
+            at_left = jnp.sum(a * y_left[p], axis=1, keepdims=True)
+            at_right = jnp.sum(a * y_right[p], axis=1, keepdims=True)
+            ends = pltpu.roll(ends, 1, 1)
+            ends = jnp.where(lane == 0, at_left, jnp.where(lane == SUB, at_right, ends))
+        return ends
+
+    ends = lax.fori_loop(0, ncomp, add_ends, jnp.zeros((nx, ny), jnp.float32)).T
     il, ir = ends[:SUB], ends[SUB : 2 * SUB]
     y_copies = [
         copy(yr_send.at[peer], yr_recv.at[iy], ys.at[o], yr.at[o], {"gy": peer})
@@ -389,13 +407,17 @@
     ]
     ends_send(yr_send, il, ir, y_first, y_last, y_copies)
 
-    for f in range(nf):
-        scr[f // planes, f % planes] = middle[f].T
-    m = jnp.stack([scr[:, :, pl.ds(t, SUB, stride=ty), :] for t in range(ty)])
-    w = inner_part(m, yt, yrow, row_y, wide)
-    for t in range(ty):
-        scr[:, :, pl.ds(t, SUB, stride=ty), :] = w[t]
-    w = [scr[f // planes, f % planes].T for f in range(nf)]
+    @pl.loop(0, ncomp)
+    def _(c):
+        for p in range(planes):
+            scr[c, p] = src[c, :, p].reshape(nx, ny).T
+        m = jnp.stack([scr[c, :, pl.ds(t, SUB, stride=ty), :] for t in range(ty)])
+        w = inner_part(m, yt, yrow, row_y, same)
+        for t in range(ty):
+            scr[c, :, pl.ds(t, SUB, stride=ty), :] = w[t]
+        for p in range(planes):
+            src[c, :, p] = scr[c, p].T.reshape(tx, SUB, ny)
+
     for c, sends, takes in halos:
         pl.when(sends)(c.wait_send)
     for c in xm_copies + ym_copies + x_copies + y_copies:
@@ -406,12 +428,17 @@
     low, high = ends_solve(yr_recv, il, ir, y_inner, dy, iy)
     blank = jnp.zeros((ny - 2 * SUB, nx), jnp.float32)
     ends = jnp.concatenate([low, high, blank], 0).T
-    for f in range(nf):
-        p = f % planes
-        a = w[f] + y_left[p] * ends[:, f : f + 1] + y_right[p] * ends[:, SUB + f : SUB + f + 1]
-        a = a.reshape(tx, SUB, ny)
-        for t in range(tx):
-            out[f // planes, p, pl.ds(t, SUB, stride=tx), :] = a[t]
+
+    def finish(c, ends):
+        for p in range(planes):
+            a = y_left[p] * ends[:, 0:1] + y_right[p] * ends[:, SUB : SUB + 1]
+            a = src[c, :, p] + a.reshape(tx, SUB, ny)
+            for t in range(tx):
+                out[c, p, pl.ds(t, SUB, stride=tx), :] = a[t]
+            ends = pltpu.roll(ends, ny - 1, 1)
+        return ends
+
+    lax.fori_loop(0, ncomp, finish, ends)
 
 
 def local(dx, dy, velocity, diffusion):
@@ -439,6 +466,9 @@
             pltpu.VMEM((dy, SUB, nx), f32),
             pltpu.VMEM((ncomp, planes, ny, nx), f32),
             pltpu.VMEM((planes, ny, nx), f32),
+            pltpu.VMEM((nx // SUB, ncomp, planes, SUB, ny), f32),
+            pltpu.VMEM((ncomp, nx // SUB, planes, SUB, ny), f32),
+            pltpu.VMEM((2, SUB, ny), f32),
             dma((2,)), dma((4,)), dma((4,)),
             dma((dx,)), dma((dx,)), dma((dx,)), dma((dx,)),
             dma((dy,)), dma((dy,)), dma((dy,)), dma((dy,)),

time: 18 us -> 19.1 us (1.061)
  Pallas kernels: 17.1 us -> 18.2 us
    pallas_call x1, Pallas kernels: 17.1 us -> 18.2 us  [local(): pl.pallas_call(functools.partial(kernel, dx, dy), out_shape=pltpu.VMEM(ve...]
where the time goes in v7:
time: 19.1 us; the launch traced here: 18.9 us
  Pallas kernels  18.2 us (95%)
  local copies, waits for them, and re-layouts  0.75 us (4%)
    pallas_call x1, Pallas kernels, local(): pl.pallas_call(functools.partial(kernel, dx, dy), out_shape=pltpu.VMEM(ve...  18.2 us
    unnamed x1, local copies, waits for them, and re-layouts  0.75 us

profile of v7, /device:TPU:0, one launch (start us, length us, event | category | flops | bytes accessed | tf_op | source)
XLA Modules:
  0.0 18.9 jit_solution(16019909281938402764)
XLA Ops:
  0.0 18.2 %shard_map.28 = f32[3,2,128,128]{3,2,1,0:T(8,128)S(1)} custom-call(f32[3,2,128,128]{3,2,1,0:T(8,128)} %vel_in.1, f32[2,128,128]{2,1,0:T(8,128)} %dif_in.1), custom_call_target="tpu_custom_call" | custom-call | tf_op jit(solution)/shard_map/pallas_call | solution.py:449
  18.2 0.7 %copy.4 = f32[3,2,128,128]{3,2,1,0:T(8,128)} copy(f32[3,2,128,128]{3,2,1,0:T(8,128)S(1)} %shard_map.28) | data formatting | bytes 786432

commit v8 on v5

--- a/solution.py
+++ b/solution.py
@@ -114,6 +114,15 @@
     m = solve(0, wl, wr)
     w = jnp.where(row % 2 == 1, wr, roll_rows(m, 7))
     return jnp.where(row == 0, left, roll_rows(w, 1)), w
+
+
+def end_shapes(levels, row_levels, row):
+    one = jnp.ones_like(row_levels[0][0])
+    out = []
+    for left, right in ((one, 0.0 * one), (0.0 * one, one)):
+        low, high = rows_down(left, right, row_levels, [0.0] * 3, row)
+        out.append(tree_down(low, high, levels, [0.0] * len(levels), lambda a: a))
+    return out
 
 
 def pick(place, items):
@@ -191,7 +200,7 @@
         c.start()
 
 
-def ends_solve(recv, il, ir, inner, count, place, ncomp, planes):
+def ends_solve(recv, il, ir, inner, count, place):
     for k in range(count):
         tile = recv[k]
         il = il + jnp.where(k < place, tile, 0.0)
@@ -199,11 +208,7 @@
     low = inner[0] * il + inner[1] * ir
     high = inner[1] * il + inner[2] * ir
 
-    def split(a):
-        parts = [jnp.broadcast_to(a[f : f + 1], a.shape) for f in range(ncomp * planes)]
-        return jnp.stack(parts).reshape((ncomp, planes) + a.shape)
-
-    return split(low), split(high)
+    return low, high
 
 
 def kernel(
@@ -346,9 +351,20 @@
         c.wait_recv()
     y_first, y_last, y_inner = ends_matrix(ym, dy, iy, planes, row_y)
 
+    shapes = []
+    for shape in end_shapes(yt, yrow, row_y):
+        for t in range(ty):
+            scr_d[:, pl.ds(t, SUB, stride=ty), :] = shape[t]
+        shapes.append([scr_d[p].T for p in range(planes)])
+    y_left, y_right = shapes
+
+    def split(a):
+        parts = [jnp.broadcast_to(a[f : f + 1], a.shape) for f in range(nf)]
+        return jnp.stack(parts).reshape((ncomp, planes) + a.shape)
+
     for c in x_copies:
         c.wait_recv()
-    low, high = ends_solve(xr_recv, il, ir, x_inner, dx, ix, ncomp, planes)
+    low, high = (split(a) for a in ends_solve(xr_recv, il, ir, x_inner, dx, ix))
     left, right = rows_down(low, high, xrow, xrowmids, row)
     middle = tree_down(left, right, xt, xmids, wide)
 
@@ -364,22 +380,29 @@
         for o, peer in enumerate(y_peers)
     ]
     ends_send(yr_send, il, ir, y_first, y_last, y_copies)
+
+    zero = jnp.zeros_like(m[0])
+    left, right = rows_down(zero, zero, yrow, yrowmids, row_y)
+    w = tree_down(left, right, yt, ymids, wide)
+    for t in range(ty):
+        scr[:, :, pl.ds(t, SUB, stride=ty), :] = w[t]
+    w = [scr[f // planes, f % planes].T for f in range(nf)]
     for c, sends, takes in halos:
         pl.when(sends)(c.wait_send)
     for c in xm_copies + ym_copies + x_copies + y_copies:
         c.wait_send()
+
     for c in y_copies:
         c.wait_recv()
-    low, high = ends_solve(yr_recv, il, ir, y_inner, dy, iy, ncomp, planes)
-    left, right = rows_down(low, high, yrow, yrowmids, row_y)
-    w = tree_down(left, right, yt, ymids, wide)
-    for t in range(ty):
-        scr[:, :, pl.ds(t, SUB, stride=ty), :] = w[t]
+    low, high = ends_solve(yr_recv, il, ir, y_inner, dy, iy)
+    blank = jnp.zeros((ny - 2 * SUB, nx), jnp.float32)
+    ends = jnp.concatenate([low, high, blank], 0).T
     for f in range(nf):
-        cc, p = f // planes, f % planes
-        a = scr[cc, p].T.reshape(tx, SUB, ny)
+        p = f % planes
+        a = w[f] + y_left[p] * ends[:, f : f + 1] + y_right[p] * ends[:, SUB + f : SUB + f + 1]
+        a = a.reshape(tx, SUB, ny)
         for t in range(tx):
-            out[cc, p, pl.ds(t, SUB, stride=tx), :] = a[t]
+            out[f // planes, p, pl.ds(t, SUB, stride=tx), :] = a[t]
 
 
 def local(dx, dy, velocity, diffusion):

time: 17.9 us -> 18 us (level)
  no operation moved by 1% of the time
where the time goes in v8:
time: 18 us; the launch traced here: 17.9 us
  Pallas kernels  17.1 us (95%)
  local copies, waits for them, and re-layouts  0.75 us (4%)
    pallas_call x1, Pallas kernels, local(): pl.pallas_call(functools.partial(kernel, dx, dy), out_shape=pltpu.VMEM(ve...  17.1 us
    unnamed x1, local copies, waits for them, and re-layouts  0.75 us

profile of v8, /device:TPU:0, one launch (start us, length us, event | category | flops | bytes accessed | tf_op | source)
XLA Modules:
  0.0 17.9 jit_solution(14618733679904411081)
XLA Ops:
  0.0 17.1 %shard_map.28 = f32[3,2,128,128]{3,2,1,0:T(8,128)S(1)} custom-call(f32[3,2,128,128]{3,2,1,0:T(8,128)} %vel_in.1, f32[2,128,128]{2,1,0:T(8,128)} %dif_in.1), custom_call_target="tpu_custom_call" | custom-call | tf_op jit(solution)/shard_map/pallas_call | solution.py:413
  17.1 0.7 %copy.4 = f32[3,2,128,128]{3,2,1,0:T(8,128)} copy(f32[3,2,128,128]{3,2,1,0:T(8,128)S(1)} %shard_map.28) | data formatting | bytes 786432

commit v9 on v5

--- a/solution.py
+++ b/solution.py
@@ -217,7 +217,7 @@
     nf = ncomp * planes
     ix, iy = lax.axis_index("gx"), lax.axis_index("gy")
     x_peers = [lax.rem(ix + o, dx) for o in range(1, dx)]
-    y_peers = [lax.rem(iy + o, dy) for o in range(1, dy)]
+    y_peers = [lax.rem(iy + o, dy) for o in sorted(range(1, dy), key=lambda o: abs(2 * o - dy))]
 
     vel_copy = pltpu.make_async_copy(vel_in, vel, ins.at[0])
     dif_copy = pltpu.make_async_copy(dif_in, dif, ins.at[1])

time: 17.9 us -> 18 us (level)
  no operation moved by 1% of the time
where the time goes in v9:
time: 18 us; the launch traced here: 17.8 us
  Pallas kernels  17.1 us (95%)
  local copies, waits for them, and re-layouts  0.75 us (4%)
    pallas_call x1, Pallas kernels, local(): pl.pallas_call(functools.partial(kernel, dx, dy), out_shape=pltpu.VMEM(ve...  17.1 us
    unnamed x1, local copies, waits for them, and re-layouts  0.75 us

profile of v9, /device:TPU:0, one launch (start us, length us, event | category | flops | bytes accessed | tf_op | source)
XLA Modules:
  0.0 17.8 jit_solution(9222083851973617328)
XLA Ops:
  0.0 17.1 %shard_map.28 = f32[3,2,128,128]{3,2,1,0:T(8,128)S(1)} custom-call(f32[3,2,128,128]{3,2,1,0:T(8,128)} %vel_in.1, f32[2,128,128]{2,1,0:T(8,128)} %dif_in.1), custom_call_target="tpu_custom_call" | custom-call | tf_op jit(solution)/shard_map/pallas_call | solution.py:390
  17.1 0.7 %copy.4 = f32[3,2,128,128]{3,2,1,0:T(8,128)} copy(f32[3,2,128,128]{3,2,1,0:T(8,128)S(1)} %shard_map.28) | data formatting | bytes 786432
